TPU v7x, 1024 devices: a whole 4x8x16 slice. The times are simulated.
1024 devices in a mesh: replica: 4 (over y_hi, core), fsdp: 256 (over y_lo, z, x).
Axes of the slice: x: 4, y: 8 (y_hi: 2, y_lo: 4; y = y_hi * 4 + y_lo), z: 16, core: 2. Of those that a mesh axis runs over, the one named last changes fastest.
Arguments:
- tokens: bfloat16 [4, 49152, 4096], P('replica', 'fsdp'), may hold values from -6 to 6
- gain: float32 [4, 4096], P('replica'), may hold values from 0.5 to 1.5
- key_cotangent: bfloat16 [4, 49152, 512], P('replica', 'fsdp'), may hold values from -6 to 6
- global_params: float32 [4096, 512], P('fsdp'), may hold values from -0.09375 to 0.09375
- local_params: bfloat16 [4, 4096, 512], P('replica', 'fsdp'), may hold values from -0.09375 to 0.09375
- momentum: float32 [4096, 512], P('fsdp'), may hold values from -0.06 to 0.06
- sign_bits: int32 [512], replicated, may hold values from 0 to 1
Outputs:
- key_out: bfloat16 [4, 49152, 512], P('replica', 'fsdp')
- grad_tokens: bfloat16 [4, 49152, 4096], P('replica', 'fsdp')
- new_params: float32 [4096, 512], P('fsdp')
- new_momentum: float32 [4096, 512], P('fsdp')
All inputs are finite; a program needn't handle non-finite values. Where the computation divides by a largest or mean magnitude, that divisor is 1e-20 or more.
Results may differ from a plain program's by a relative error of at most 0.023.
Values may be sent and summed in bfloat16 or wider, within the bound.
No kernel may reach another device: no remote copies, remote signals or barrier semaphores. Data moves between devices by JAX's collectives and lax.ppermute only.
A program may use at most 32 MiB of HBM per device.

v0:
```python
import math

import jax
import jax.numpy as jnp
import numpy as np
from jax import lax
from jax.sharding import PartitionSpec as P

HB = 128


NORM_EPS = 1e-06
OUTER_MU = 0.9
OUTER_LR = 0.7
CLIP_LEVEL = 2.0


def hadamard(order):
    counter = np.arange(order)
    common = counter[:, None] & counter[None, :]
    parity = common & 0
    shift = 0
    while 1 << shift < order:
        parity = parity ^ common >> shift & 1
        shift = shift + 1
    return jnp.asarray((1 - 2 * parity) / math.sqrt(order), dtype=jnp.float32)


def rotate(values, sign_vec):
    width = values.shape[-1]
    blocks = (values * sign_vec).reshape(values.shape[:-1] + (width // HB, HB))
    return jnp.einsum("...bi,ij->...bj", blocks, hadamard(HB), precision=lax.Precision.HIGHEST)


def clip_terms(rotated):
    block_scale = jnp.mean(jnp.abs(rotated), axis=-1, keepdims=True) + NORM_EPS
    return jnp.clip(rotated / block_scale, -CLIP_LEVEL, CLIP_LEVEL) * block_scale


def outer_update(global_rows, moment_rows, averaged, sign_vec):
    row_count, width = global_rows.shape
    blocks = averaged.reshape(row_count, width // HB, HB)
    restored = jnp.einsum("rbi,ij->rbj", blocks, hadamard(HB), precision=lax.Precision.HIGHEST)
    pseudo = restored.reshape(row_count, width) * sign_vec
    fresh_moment = OUTER_MU * moment_rows + pseudo
    fresh_params = global_rows - OUTER_LR * (pseudo + OUTER_MU * fresh_moment)
    return (fresh_params, fresh_moment)


def body(tokens, gain, key_cotangent, global_params, local_params, momentum, sign_bits):
    sign_vec = (2 * sign_bits - 1).astype(jnp.float32)
    drift = global_params - local_params[0].astype(jnp.float32)
    row_count, width = drift.shape
    terms = clip_terms(rotate(drift, sign_vec)).reshape(row_count, width)
    replicas = lax.axis_size("replica")
    summed = lax.psum(terms.astype(jnp.bfloat16), "replica").astype(jnp.float32)
    new_params, new_momentum = outer_update(global_params, momentum, summed / replicas, sign_vec)
    weight_part = new_params.astype(jnp.bfloat16)
    tok_float = tokens[0].astype(jnp.float32)
    gain_vec = gain[0]
    cotangent = key_cotangent[0]
    inverse = lax.rsqrt(jnp.mean(tok_float * tok_float, axis=-1, keepdims=True) + NORM_EPS)
    normed = tok_float * inverse
    hidden = (normed * gain_vec).astype(jnp.bfloat16)
    keys = jnp.dot(
        hidden,
        lax.all_gather(weight_part, "fsdp", axis=0, tiled=True),
        preferred_element_type=jnp.float32,
    )
    back = lax.dot_general(
        cotangent,
        lax.all_gather(weight_part, "fsdp", axis=0, tiled=True),
        (((1,), (1,)), ((), ())),
        preferred_element_type=jnp.float32,
    )
    scaled = back * gain_vec
    centre = jnp.mean(scaled * normed, axis=-1, keepdims=True)
    grads = (inverse * (scaled - normed * centre)).astype(jnp.bfloat16)
    key_out = keys.astype(jnp.bfloat16)[None]
    grad_tokens = grads[None]
    return (key_out, grad_tokens, new_params, new_momentum)


def solution(mesh):
    in_specs = (
        P("replica", "fsdp", None),
        P("replica", None),
        P("replica", "fsdp", None),
        P("fsdp", None),
        P("replica", "fsdp", None),
        P("fsdp", None),
        P(),
    )
    out_specs = (
        P("replica", "fsdp", None),
        P("replica", "fsdp", None),
        P("fsdp", None),
        P("fsdp", None),
    )
    return jax.shard_map(body, mesh=mesh, in_specs=in_specs, out_specs=out_specs, check_vma=False)
```

profile of v0, /device:TPU:32, one launch (start us, length us, event | category | flops | bytes accessed | tf_op | source)
XLA Modules:
  0.0 1423.6 jit_solution(15084331077709485939)
XLA Ops:
  7.2 0.0 copy-start
  7.2 0.0 all-gather.2.cloned.1.call-start
  7.2 0.7 add_convert_fusion
  8.0 1.1 abs_reduce_fusion
  9.1 0.1 copy_bitcast_fusion
  9.2 24.6 %psum.7 = bf16[16,512]{1,0:T(8,128)(2,1)S(1)} all-reduce(bf16[16,512]{1,0:T(8,128)(2,1)S(1)} %copy_bitcast_fusion), channel_id=1, replica_groups=mesh['replica'=4,'fsdp'=256] {'replica'}, use_global_device_ids=true, to_apply=%region_2.3 | all-reduce | flops 8192 | bytes 32768 | tf_op jit(solution)/shard_map/psum | solution.py:56
  33.8 1.0 convolution_bitcast_fusion
  34.8 1.4 fusion.31
  36.2 0.0 all-gather.2.cloned.1.call-update
  36.2 1.8 fusion.9
  38.0 1369.8 %all-gather.2.cloned.1.call-done = bf16[4096,512]{1,0:T(8,128)(2,1)} async-done(((bf16[16,512]{1,0:T(8,128)(2,1)}), bf16[4096,512]{1,0:T(8,128)(2,1)}) %all-gather.2.cloned.1.call-update) | async-done | bytes 4194320 | tf_op jit(solution)/shard_map/all_gather | solution.py:67
  1407.8 0.0 copy-done
  1407.8 0.0 copy-start.1
  1407.8 4.4 fusion.5
  1412.3 0.0 copy-done.1
  1412.3 0.0 copy-start.2
  1412.3 0.0 copy-start.3
  1412.3 1.9 fusion.10
  1414.2 0.8 copy-done.2
  1415.1 0.0 copy-done.3
  1415.1 1.7 fusion.19
  (3 shorter events, 0.0 us)
Async XLA Ops:
  7.2 1400.7 %copy-start = (bf16[1,192,512]{2,1,0:T(8,128)(2,1)S(1)}, bf16[1,192,512]{2,1,0:T(8,128)(2,1)}, u32[]{:S(2)}) copy-start(bf16[1,192,512]{2,1,0:T(8,128)(2,1)} %param.11) | copy-start | bytes 589828
  7.2 1400.7 %all-gather.2.cloned.1.call-start = ((), (), s32[]{:S(2)}) async-start(), calls=%async_computation | async-start | bytes 4210688 | tf_op jit(solution)/shard_map/all_gather | solution.py:67
  1407.8 4.5 copy-start.1
  1412.3 2.8 copy-start.2
  1412.3 2.7 copy-start.3
Sparse Core Ops, SparseCore 0:
  36.3 1371.4 all-gather.1
where the time goes:
time: 1420 us
  waiting for transfers between devices  1370 us (96%)
  blocking collectives  24.6 us (2%)
    all_gather x1, waiting for transfers between devices, body(): lax.all_gather(weight_part, 'fsdp', axis=0, tiled=True)  1370 us
  transfers between devices with their start and end apart: 1, of which 1 were waited for; matrix products, arithmetic and copies ran while one was open for 0% of the time, Pallas kernels for 0%

commit v1 on v0

--- a/solution.py
+++ b/solution.py
@@ -4,7 +4,7 @@
 import jax.numpy as jnp
 import numpy as np
 from jax import lax
-from jax.sharding import PartitionSpec as P
+from jax.sharding import Mesh, PartitionSpec as P
 
 HB = 128
 
@@ -13,6 +13,10 @@
 OUTER_MU = 0.9
 OUTER_LR = 0.7
 CLIP_LEVEL = 2.0
+
+REPLICA = ("yh", "core")
+FSDP = ("yl", "zh", "zl", "x")
+SIZES = {"yh": 2, "core": 2, "yl": 4, "zh": 4, "zl": 4, "x": 4}
 
 
 def hadamard(order):
@@ -47,32 +51,44 @@
     return (fresh_params, fresh_moment)
 
 
+def gather(block, axes):
+    count = math.prod(SIZES[axis] for axis in axes)
+    copies = jnp.broadcast_to(block[None], (count,) + block.shape)
+    return lax.all_to_all(copies, axes, 0, 0, tiled=True)
+
+
 def body(tokens, gain, key_cotangent, global_params, local_params, momentum, sign_bits):
     sign_vec = (2 * sign_bits - 1).astype(jnp.float32)
     drift = global_params - local_params[0].astype(jnp.float32)
     row_count, width = drift.shape
-    terms = clip_terms(rotate(drift, sign_vec)).reshape(row_count, width)
-    replicas = lax.axis_size("replica")
-    summed = lax.psum(terms.astype(jnp.bfloat16), "replica").astype(jnp.float32)
+    terms = clip_terms(rotate(drift, sign_vec)).reshape(row_count, width).astype(jnp.bfloat16)
+    all_terms = gather(terms, REPLICA)
+    replicas = all_terms.shape[0]
+    summed = jnp.sum(all_terms.astype(jnp.float32), axis=0)
     new_params, new_momentum = outer_update(global_params, momentum, summed / replicas, sign_vec)
     weight_part = new_params.astype(jnp.bfloat16)
+
+    half = width // 2
+    core = lax.axis_index("core")
+    mine = jnp.where(core == 0, weight_part[:, :half], weight_part[:, half:])
+    got = gather(mine, ("zh",))
+    got = gather(got, ("yl", "zl"))
+    got = gather(got, ("x",))
+    got = got.reshape(4, 4, 4, 4, row_count, half).transpose(1, 3, 2, 0, 4, 5)
+    got = got.reshape(-1, half)
+    other = lax.ppermute(got, "core", [(0, 1), (1, 0)])
+    low = jnp.where(core == 0, got, other)
+    high = jnp.where(core == 0, other, got)
+    weight = jnp.concatenate([low, high], axis=1)
+
     tok_float = tokens[0].astype(jnp.float32)
     gain_vec = gain[0]
     cotangent = key_cotangent[0]
     inverse = lax.rsqrt(jnp.mean(tok_float * tok_float, axis=-1, keepdims=True) + NORM_EPS)
     normed = tok_float * inverse
     hidden = (normed * gain_vec).astype(jnp.bfloat16)
-    keys = jnp.dot(
-        hidden,
-        lax.all_gather(weight_part, "fsdp", axis=0, tiled=True),
-        preferred_element_type=jnp.float32,
-    )
-    back = lax.dot_general(
-        cotangent,
-        lax.all_gather(weight_part, "fsdp", axis=0, tiled=True),
-        (((1,), (1,)), ((), ())),
-        preferred_element_type=jnp.float32,
-    )
+    keys = jnp.dot(hidden, weight, preferred_element_type=jnp.float32)
+    back = lax.dot_general(cotangent, weight, (((1,), (1,)), ((), ())), preferred_element_type=jnp.float32)
     scaled = back * gain_vec
     centre = jnp.mean(scaled * normed, axis=-1, keepdims=True)
     grads = (inverse * (scaled - normed * centre)).astype(jnp.bfloat16)
@@ -82,19 +98,20 @@
 
 
 def solution(mesh):
+    fine = Mesh(mesh.devices.reshape(tuple(SIZES.values())), tuple(SIZES))
     in_specs = (
-        P("replica", "fsdp", None),
-        P("replica", None),
-        P("replica", "fsdp", None),
-        P("fsdp", None),
-        P("replica", "fsdp", None),
-        P("fsdp", None),
+        P(REPLICA, FSDP, None),
+        P(REPLICA, None),
+        P(REPLICA, FSDP, None),
+        P(FSDP, None),
+        P(REPLICA, FSDP, None),
+        P(FSDP, None),
         P(),
     )
     out_specs = (
-        P("replica", "fsdp", None),
-        P("replica", "fsdp", None),
-        P("fsdp", None),
-        P("fsdp", None),
+        P(REPLICA, FSDP, None),
+        P(REPLICA, FSDP, None),
+        P(FSDP, None),
+        P(FSDP, None),
     )
-    return jax.shard_map(body, mesh=mesh, in_specs=in_specs, out_specs=out_specs, check_vma=False)
+    return jax.shard_map(body, mesh=fine, in_specs=in_specs, out_specs=out_specs, check_vma=False)

time: 1420 us -> 116 us (0.08)
  the two profiles are of different devices: /device:TPU:32 before, /device:TPU:1 now
where the time goes in v1:
time: 116 us; the launch traced here: 115 us
  blocking collectives  69.7 us (60%)
  starting transfers between devices  22.7 us (20%)
  waiting for transfers between devices  10.5 us (9%)
  matrix products  5.53 us (5%)
  other arithmetic  5.04 us (4%)
  local copies, waits for them, and re-layouts  1.19 us (1%)
    all_to_all x3, blocking collectives, gather(): return lax.all_to_all(copies, axes, 0, 0, tiled=True)  69.7 us
    all_to_all x1, starting transfers between devices, gather(): return lax.all_to_all(copies, axes, 0, 0, tiled=True)  17.4 us
    all_to_all x1, waiting for transfers between devices, gather(): return lax.all_to_all(copies, axes, 0, 0, tiled=True)  7.17 us
    ppermute x1, starting transfers between devices, body(): other = lax.ppermute(got, 'core', [(0, 1), (1, 0)])  5.29 us
    ppermute x1, waiting for transfers between devices, body(): other = lax.ppermute(got, 'core', [(0, 1), (1, 0)])  3.34 us
  transfers between devices with their start and end apart: 2, of which 2 were waited for; matrix products, arithmetic and copies ran while one was open for 0% of the time, Pallas kernels for 0%

profile of v1, /device:TPU:1, one launch (start us, length us, event | category | flops | bytes accessed | tf_op | source)
XLA Modules:
  0.0 115.4 jit_solution(7865996843176616270)
XLA Ops:
  0.6 0.0 copy-start
  0.6 0.7 add_convert_fusion
  1.4 1.1 abs_reduce_fusion
  2.5 0.1 copy_bitcast_fusion
  2.6 0.6 broadcast_in_dim.12
  3.3 17.4 %all-to-all-start = ((bf16[4,16,512]{2,1,0:T(8,128)(2,1)}), bf16[4,16,512]{2,1,0:T(8,128)(2,1)S(1)}, u32[]{:S(2)}, u32[]{:S(2)}) async-start(bf16[4,16,512]{2,1,0:T(8,128)(2,1)} %broadcast_in_dim.12), calls=%async_computation | async-start | bytes 131072 | tf_op jit(solution)/shard_map/all_to_all | solution.py:57
  20.7 7.2 %all-to-all-done = bf16[4,16,512]{2,1,0:T(8,128)(2,1)S(1)} async-done(((bf16[4,16,512]{2,1,0:T(8,128)(2,1)}), bf16[4,16,512]{2,1,0:T(8,128)(2,1)S(1)}, u32[]{:S(2)}, u32[]{:S(2)}) %all-to-all-start) | async-done | bytes 65568 | tf_op jit(solution)/shard_map/all_to_all | solution.py:57
  27.8 1.0 convolution_bitcast_fusion
  28.9 1.4 %fusion.33 = (bf16[16,512]{1,0:T(8,128)(2,1)S(1)}, f32[16,512]{1,0:T(8,128)}, f32[16,512]{1,0:T(8,128)}) fusion(f32[16,512]{1,0:T(8,128)} %param.12, f32[512]{0:T(512)S(1)} %add_convert_fusion, f32[4,2,8,128]{3,2,1,0:T(8,128)S(1)} %convolution_bitcast_fusion, f32[16,512]{1,0:T(8,128)} %param.14), kind=kLoop, calls=%fused_computation.49 | loop fusion | flops 65536 | bytes 182272 | tf_op jit(solution)/shard_map/convert_element_type | solution.py:69
  30.3 21.5 %all_to_all.20 = bf16[4,16,256]{2,1,0:T(8,128)(2,1)S(1)} all-to-all(bf16[4,16,256]{2,1,0:T(8,128)(2,1)S(1)} %broadcast_in_dim.13), channel_id=1, replica_groups=mesh['yh'=2,'core'=2,'yl'=4,'zh'=4,'zl'=4,'x'=4] {'zh'}, dimensions={0} | all-to-all | bytes 65536 | tf_op jit(solution)/shard_map/all_to_all | solution.py:57
  51.8 20.4 %all_to_all.21 = bf16[16,4,16,256]{3,2,1,0:T(8,128)(2,1)S(1)} all-to-all(bf16[16,4,16,256]{3,2,1,0:T(8,128)(2,1)S(1)} %broadcast_in_dim.14), channel_id=1, replica_groups=mesh['yh'=2,'core'=2,'yl'=4,'zh'=4,'zl'=4,'x'=4] {'yl','zl'}, dimensions={0} | all-to-all | bytes 1048576 | tf_op jit(solution)/shard_map/all_to_all | solution.py:57
  72.2 0.2 broadcast_in_dim.15
  72.5 27.8 %all_to_all.22 = bf16[4,16,4,16,256]{4,3,2,1,0:T(8,128)(2,1)S(1)} all-to-all(bf16[4,16,4,16,256]{4,3,2,1,0:T(8,128)(2,1)S(1)} %broadcast_in_dim.15), channel_id=1, replica_groups=mesh['yh'=2,'core'=2,'yl'=4,'zh'=4,'zl'=4,'x'=4] {'x'}, dimensions={0} | all-to-all | bytes 4194304 | tf_op jit(solution)/shard_map/all_to_all | solution.py:57
  100.3 0.0 copy-start.1
  100.3 0.2 copy.27
  100.6 5.3 %collective-permute-start = (bf16[4096,256]{1,0:T(8,128)(2,1)S(1)}, bf16[4096,256]{1,0:T(8,128)(2,1)S(1)}, u32[]{:S(2)}, u32[]{:S(2)}) collective-permute-start(bf16[4096,256]{1,0:T(8,128)(2,1)S(1)} %bitcast.71), channel_id=1, source_target_pairs={{0,256},{256,0},{1,257},{257,1},{2,258},{258,2},{3,259},{259,3},{4... | collective-permute-start | bytes 6291464 | tf_op jit(solution)/shard_map/ppermute | solution.py:79
  105.9 0.0 copy-done.1
  105.9 0.4 fusion.9
  106.3 0.0 copy-start.2
  106.3 3.3 %collective-permute-done = bf16[4096,256]{1,0:T(8,128)(2,1)S(1)} collective-permute-done((bf16[4096,256]{1,0:T(8,128)(2,1)S(1)}, bf16[4096,256]{1,0:T(8,128)(2,1)S(1)}, u32[]{:S(2)}, u32[]{:S(2)}) %collective-permute-start) | collective-permute-done | bytes 2097184 | tf_op jit(solution)/shard_map/ppermute | solution.py:79
  109.6 0.4 broadcast_select_fusion.1
  110.0 0.0 copy-done.2
  110.0 1.7 %fusion.19 = bf16[1,192,512]{2,1,0:T(8,128)(2,1)} fusion(bf16[4096,256]{1,0:T(8,128)(2,1)S(1)} %get-tuple-element.8, bf16[4096,256]{1,0:T(8,128)(2,1)S(1)} %get-tuple-element.7, bf16[1,192,4096]{2,1,0:T(8,128)(2,1)S(1)} %copy-done.1, f32[4096]{0:T(1024)S(1)} %bitcast.72, f32[192]{0:T(256)S(1)} %add_rsqrt_fusion), kind=kOutput, calls=%fused_computation.22 | convolution fusion | flops 816939008 | bytes 5980928 | tf_op jit(solution)/shard_map/dot_general | solution.py:90
  111.8 0.0 copy-done
  111.8 1.7 %fusion.5 = (f32[192]{0:T(256)S(1)}, f32[192,4096]{1,0:T(8,128)S(1)}) fusion(bf16[1,192,4096]{2,1,0:T(8,128)(2,1)S(1)} %copy-done.1, f32[192]{0:T(256)S(1)} %add_rsqrt_fusion, f32[4096]{0:T(1024)S(1)} %bitcast.73, bf16[1,192,512]{2,1,0:T(8,128)(2,1)S(1)} %copy-done, bf16[4096,256]{1,0:T(8,128)(2,1)S(1)} %get-tuple-element.8, ...), kind=kOutput, calls=%fused_computation.9 | convolution fusion | flops 817626944 | bytes 9127424 | tf_op jit(solution)/shard_map/dot_general | solution.py:91
  113.4 2.0 %fusion.11 = bf16[1,192,4096]{2,1,0:T(8,128)(2,1)} fusion(f32[192,4096]{1,0:T(8,128)S(1)} %get-tuple-element.12, bf16[1,192,4096]{2,1,0:T(8,128)(2,1)S(1)} %copy-done.1, f32[192]{0:T(256)S(1)} %broadcast_multiply_fusion, f32[192]{0:T(256)S(1)} %add_rsqrt_fusion), kind=kLoop, calls=%fused_computation.17 | loop fusion | flops 4718592 | bytes 6292992 | tf_op jit(solution)/shard_map/broadcast_in_dim | solution.py:96
  (7 shorter events, 0.1 us)
Async XLA Ops:
  0.6 111.1 %copy-start = (bf16[1,192,512]{2,1,0:T(8,128)(2,1)S(1)}, bf16[1,192,512]{2,1,0:T(8,128)(2,1)}, u32[]{:S(2)}) copy-start(bf16[1,192,512]{2,1,0:T(8,128)(2,1)} %param.11) | copy-start | bytes 589828
  3.3 24.6 %all-to-all-start = ((bf16[4,16,512]{2,1,0:T(8,128)(2,1)}), bf16[4,16,512]{2,1,0:T(8,128)(2,1)S(1)}, u32[]{:S(2)}, u32[]{:S(2)}) async-start(bf16[4,16,512]{2,1,0:T(8,128)(2,1)} %broadcast_in_dim.12), calls=%async_computation | async-start | bytes 131072 | tf_op jit(solution)/shard_map/all_to_all | solution.py:57
  100.3 5.6 %copy-start.1 = (bf16[1,192,4096]{2,1,0:T(8,128)(2,1)S(1)}, bf16[1,192,4096]{2,1,0:T(8,128)(2,1)}, u32[]{:S(2)}) copy-start(bf16[1,192,4096]{2,1,0:T(8,128)(2,1)} %param.9) | copy-start | bytes 4718596
  100.6 9.1 %collective-permute-start = (bf16[4096,256]{1,0:T(8,128)(2,1)S(1)}, bf16[4096,256]{1,0:T(8,128)(2,1)S(1)}, u32[]{:S(2)}, u32[]{:S(2)}) collective-permute-start(bf16[4096,256]{1,0:T(8,128)(2,1)S(1)} %bitcast.71), channel_id=1, source_target_pairs={{0,256},{256,0},{1,257},{257,1},{2,258},{258,2},{3,259},{259,3},{4... | collective-permute-start | bytes 6291464 | tf_op jit(solution)/shard_map/ppermute | solution.py:79
  106.3 3.8 %copy-start.2 = (f32[1,4096]{1,0:T(1,128)S(1)}, f32[1,4096]{1,0:T(1,128)}, u32[]{:S(2)}) copy-start(f32[1,4096]{1,0:T(1,128)} %param.10) | copy-start | bytes 49156

commit v2 on v1

--- a/solution.py
+++ b/solution.py
@@ -15,8 +15,8 @@
 CLIP_LEVEL = 2.0
 
 REPLICA = ("yh", "core")
-FSDP = ("yl", "zh", "zl", "x")
-SIZES = {"yh": 2, "core": 2, "yl": 4, "zh": 4, "zl": 4, "x": 4}
+FSDP = ("y1", "y0", "zh", "z0", "x")
+SIZES = {"yh": 2, "core": 2, "y1": 2, "y0": 2, "zh": 8, "z0": 2, "x": 4}
 
 
 def hadamard(order):
@@ -71,10 +71,9 @@
     half = width // 2
     core = lax.axis_index("core")
     mine = jnp.where(core == 0, weight_part[:, :half], weight_part[:, half:])
-    got = gather(mine, ("zh",))
-    got = gather(got, ("yl", "zl"))
-    got = gather(got, ("x",))
-    got = got.reshape(4, 4, 4, 4, row_count, half).transpose(1, 3, 2, 0, 4, 5)
+    got = gather(mine, ("y1", "zh"))
+    got = gather(got, ("y0", "z0", "x"))
+    got = got.reshape(2, 2, 4, 2, 8, row_count, half).transpose(3, 0, 4, 1, 2, 5, 6)
     got = got.reshape(-1, half)
     other = lax.ppermute(got, "core", [(0, 1), (1, 0)])
     low = jnp.where(core == 0, got, other)

time: 116 us -> 101 us (0.87)
  blocking collectives: 69.7 us -> 55.2 us
    all_to_all x3 -> x2, blocking collectives: 69.7 us -> 55.2 us  [gather(): return lax.all_to_all(copies, axes, 0, 0, tiled=True)]
where the time goes in v2:
time: 101 us
  blocking collectives  55.2 us (55%)
  starting transfers between devices  22.7 us (22%)
  waiting for transfers between devices  10.5 us (10%)
  matrix products  5.53 us (5%)
  other arithmetic  5.04 us (5%)
  local copies, waits for them, and re-layouts  1.1 us (1%)
    all_to_all x2, blocking collectives, gather(): return lax.all_to_all(copies, axes, 0, 0, tiled=True)  55.2 us
    all_to_all x1, starting transfers between devices, gather(): return lax.all_to_all(copies, axes, 0, 0, tiled=True)  17.4 us
    all_to_all x1, waiting for transfers between devices, gather(): return lax.all_to_all(copies, axes, 0, 0, tiled=True)  7.17 us
    ppermute x1, starting transfers between devices, body(): other = lax.ppermute(got, 'core', [(0, 1), (1, 0)])  5.27 us
    ppermute x1, waiting for transfers between devices, body(): other = lax.ppermute(got, 'core', [(0, 1), (1, 0)])  3.34 us
  transfers between devices with their start and end apart: 2, of which 2 were waited for; matrix products, arithmetic and copies ran while one was open for 0% of the time, Pallas kernels for 0%

profile of v2, /device:TPU:1, one launch (start us, length us, event | category | flops | bytes accessed | tf_op | source)
XLA Modules:
  0.0 100.8 jit_solution(4205624888641346237)
XLA Ops:
  0.6 0.0 copy-start
  0.6 0.7 add_convert_fusion
  1.4 1.1 %abs_reduce_fusion = (f32[16,4]{0,1:T(4,128)S(1)}, f32[16,4,128]{2,0,1:T(8,128)S(1)}) fusion(f32[128,128,1]{1,0,2:T(8,128)} %constant.45, f32[16,512]{1,0:T(8,128)} %param.12, bf16[1,16,512]{2,1,0:T(8,128)(2,1)} %param.13, f32[512]{0:T(512)S(1)} %add_convert_fusion), kind=kOutput, calls=%fused_computation.39 | convolution fusion | flops 12623808 | bytes 149760 | tf_op jit(solution)/shard_map/...bi,ij->...bj/dot_general | solution.py:36
  2.5 0.1 copy_bitcast_fusion
  2.6 0.6 broadcast_in_dim.10
  3.3 17.4 %all-to-all-start = ((bf16[4,16,512]{2,1,0:T(8,128)(2,1)}), bf16[4,16,512]{2,1,0:T(8,128)(2,1)S(1)}, u32[]{:S(2)}, u32[]{:S(2)}) async-start(bf16[4,16,512]{2,1,0:T(8,128)(2,1)} %broadcast_in_dim.10), calls=%async_computation | async-start | bytes 131072 | tf_op jit(solution)/shard_map/all_to_all | solution.py:57
  20.7 7.2 %all-to-all-done = bf16[4,16,512]{2,1,0:T(8,128)(2,1)S(1)} async-done(((bf16[4,16,512]{2,1,0:T(8,128)(2,1)}), bf16[4,16,512]{2,1,0:T(8,128)(2,1)S(1)}, u32[]{:S(2)}, u32[]{:S(2)}) %all-to-all-start) | async-done | bytes 65568 | tf_op jit(solution)/shard_map/all_to_all | solution.py:57
  27.8 1.0 %convolution_bitcast_fusion = f32[4,2,8,128]{3,2,1,0:T(8,128)S(1)} fusion(f32[128,128,1]{1,0,2:T(8,128)} %constant.45, f32[16,512]{1,0:T(8,128)S(1)} %convert_reduce_fusion), kind=kOutput, calls=%fused_computation.23 | convolution fusion | flops 12591104 | bytes 131072 | tf_op jit(solution)/shard_map/rbi,ij->rbj/dot_general | solution.py:47
  28.9 1.4 %fusion.33 = (bf16[16,512]{1,0:T(8,128)(2,1)S(1)}, f32[16,512]{1,0:T(8,128)}, f32[16,512]{1,0:T(8,128)}) fusion(f32[16,512]{1,0:T(8,128)} %param.12, f32[512]{0:T(512)S(1)} %add_convert_fusion, f32[4,2,8,128]{3,2,1,0:T(8,128)S(1)} %convolution_bitcast_fusion, f32[16,512]{1,0:T(8,128)} %param.14), kind=kLoop, calls=%fused_computation.49 | loop fusion | flops 65536 | bytes 182272 | tf_op jit(solution)/shard_map/convert_element_type | solution.py:69
  30.3 23.0 %all_to_all.15 = bf16[16,16,256]{2,1,0:T(8,128)(2,1)S(1)} all-to-all(bf16[16,16,256]{2,1,0:T(8,128)(2,1)S(1)} %broadcast_in_dim.11), channel_id=1, replica_groups=mesh['yh'=2,'core'=2,'y1'=2,'y0'=2,'zh'=8,'z0'=2,'x'=4] {'y1','zh'}, dimensions={0} | all-to-all | bytes 262144 | tf_op jit(solution)/shard_map/all_to_all | solution.py:57
  53.3 0.2 broadcast_in_dim.12
  53.5 32.2 %all_to_all.16 = bf16[16,16,16,256]{3,2,1,0:T(8,128)(2,1)S(1)} all-to-all(bf16[16,16,16,256]{3,2,1,0:T(8,128)(2,1)S(1)} %broadcast_in_dim.12), channel_id=1, replica_groups=mesh['yh'=2,'core'=2,'y1'=2,'y0'=2,'zh'=8,'z0'=2,'x'=4] {'y0','z0','x'}, dimensions={0} | all-to-all | bytes 4194304 | tf_op jit(solution)/shard_map/all_to_all | solution.py:57
  85.7 0.0 copy-start.1
  85.7 0.2 copy.27
  86.0 5.3 %collective-permute-start = (bf16[4096,256]{1,0:T(8,128)(2,1)S(1)}, bf16[4096,256]{1,0:T(8,128)(2,1)S(1)}, u32[]{:S(2)}, u32[]{:S(2)}) collective-permute-start(bf16[4096,256]{1,0:T(8,128)(2,1)S(1)} %bitcast.71), channel_id=1, source_target_pairs={{0,256},{256,0},{1,257},{257,1},{2,258},{258,2},{3,259},{259,3},{4... | collective-permute-start | bytes 6291464 | tf_op jit(solution)/shard_map/ppermute | solution.py:78
  91.3 0.0 copy-done.1
  91.3 0.4 fusion.9
  91.7 0.0 copy-start.2
  91.7 3.3 %collective-permute-done = bf16[4096,256]{1,0:T(8,128)(2,1)S(1)} collective-permute-done((bf16[4096,256]{1,0:T(8,128)(2,1)S(1)}, bf16[4096,256]{1,0:T(8,128)(2,1)S(1)}, u32[]{:S(2)}, u32[]{:S(2)}) %collective-permute-start) | collective-permute-done | bytes 2097184 | tf_op jit(solution)/shard_map/ppermute | solution.py:78
  95.0 0.4 broadcast_select_fusion.1
  95.4 0.0 copy-done.2
  95.4 1.7 %fusion.19 = bf16[1,192,512]{2,1,0:T(8,128)(2,1)} fusion(bf16[4096,256]{1,0:T(8,128)(2,1)S(1)} %get-tuple-element.8, bf16[4096,256]{1,0:T(8,128)(2,1)S(1)} %get-tuple-element.7, bf16[1,192,4096]{2,1,0:T(8,128)(2,1)S(1)} %copy-done.1, f32[4096]{0:T(1024)S(1)} %bitcast.72, f32[192]{0:T(256)S(1)} %add_rsqrt_fusion), kind=kOutput, calls=%fused_computation.22 | convolution fusion | flops 816939008 | bytes 5980928 | tf_op jit(solution)/shard_map/dot_general | solution.py:89
  97.2 0.0 copy-done
  97.2 1.7 %fusion.5 = (f32[192]{0:T(256)S(1)}, f32[192,4096]{1,0:T(8,128)S(1)}) fusion(bf16[1,192,4096]{2,1,0:T(8,128)(2,1)S(1)} %copy-done.1, f32[192]{0:T(256)S(1)} %add_rsqrt_fusion, f32[4096]{0:T(1024)S(1)} %bitcast.73, bf16[1,192,512]{2,1,0:T(8,128)(2,1)S(1)} %copy-done, bf16[4096,256]{1,0:T(8,128)(2,1)S(1)} %get-tuple-element.8, ...), kind=kOutput, calls=%fused_computation.9 | convolution fusion | flops 817626944 | bytes 9127424 | tf_op jit(solution)/shard_map/dot_general | solution.py:90
  98.8 2.0 %fusion.11 = bf16[1,192,4096]{2,1,0:T(8,128)(2,1)} fusion(f32[192,4096]{1,0:T(8,128)S(1)} %get-tuple-element.12, bf16[1,192,4096]{2,1,0:T(8,128)(2,1)S(1)} %copy-done.1, f32[192]{0:T(256)S(1)} %broadcast_multiply_fusion, f32[192]{0:T(256)S(1)} %add_rsqrt_fusion), kind=kLoop, calls=%fused_computation.17 | loop fusion | flops 4718592 | bytes 6292992 | tf_op jit(solution)/shard_map/broadcast_in_dim | solution.py:95
  (6 shorter events, 0.1 us)
Async XLA Ops:
  0.6 96.5 %copy-start = (bf16[1,192,512]{2,1,0:T(8,128)(2,1)S(1)}, bf16[1,192,512]{2,1,0:T(8,128)(2,1)}, u32[]{:S(2)}) copy-start(bf16[1,192,512]{2,1,0:T(8,128)(2,1)} %param.11) | copy-start | bytes 589828
  3.3 24.6 %all-to-all-start = ((bf16[4,16,512]{2,1,0:T(8,128)(2,1)}), bf16[4,16,512]{2,1,0:T(8,128)(2,1)S(1)}, u32[]{:S(2)}, u32[]{:S(2)}) async-start(bf16[4,16,512]{2,1,0:T(8,128)(2,1)} %broadcast_in_dim.10), calls=%async_computation | async-start | bytes 131072 | tf_op jit(solution)/shard_map/all_to_all | solution.py:57
  85.7 5.5 %copy-start.1 = (bf16[1,192,4096]{2,1,0:T(8,128)(2,1)S(1)}, bf16[1,192,4096]{2,1,0:T(8,128)(2,1)}, u32[]{:S(2)}) copy-start(bf16[1,192,4096]{2,1,0:T(8,128)(2,1)} %param.9) | copy-start | bytes 4718596
  86.0 9.0 %collective-permute-start = (bf16[4096,256]{1,0:T(8,128)(2,1)S(1)}, bf16[4096,256]{1,0:T(8,128)(2,1)S(1)}, u32[]{:S(2)}, u32[]{:S(2)}) collective-permute-start(bf16[4096,256]{1,0:T(8,128)(2,1)S(1)} %bitcast.71), channel_id=1, source_target_pairs={{0,256},{256,0},{1,257},{257,1},{2,258},{258,2},{3,259},{259,3},{4... | collective-permute-start | bytes 6291464 | tf_op jit(solution)/shard_map/ppermute | solution.py:78
  91.7 3.8 %copy-start.2 = (f32[1,4096]{1,0:T(1,128)S(1)}, f32[1,4096]{1,0:T(1,128)}, u32[]{:S(2)}) copy-start(f32[1,4096]{1,0:T(1,128)} %param.10) | copy-start | bytes 49156

commit v3 on v2

--- a/solution.py
+++ b/solution.py
@@ -15,8 +15,9 @@
 CLIP_LEVEL = 2.0
 
 REPLICA = ("yh", "core")
-FSDP = ("y1", "y0", "zh", "z0", "x")
-SIZES = {"yh": 2, "core": 2, "y1": 2, "y0": 2, "zh": 8, "z0": 2, "x": 4}
+FSDP = ("y1", "y0", "zh", "z0", "x1", "x0")
+SIZES = {"yh": 2, "core": 2, "y1": 2, "y0": 2, "zh": 8, "z0": 2, "x1": 2, "x0": 2}
+AXES = tuple(SIZES)
 
 
 def hadamard(order):
@@ -51,49 +52,66 @@
     return (fresh_params, fresh_moment)
 
 
-def gather(block, axes):
-    count = math.prod(SIZES[axis] for axis in axes)
+def cubes():
+    groups = []
+    for core in range(2):
+        for y in range(0, 8, 2):
+            for z in range(0, 16, 2):
+                for x in range(0, 4, 2):
+                    group = []
+                    for odd in np.ndindex(2, 2, 2):
+                        step = [bit * (1 - 2 * core) for bit in odd]
+                        y_at, z_at, x_at = (y + step[0]) % 8, (z + step[1]) % 16, (x + step[2]) % 4
+                        group.append((((y_at // 4 * 2 + core) * 4 + y_at % 4) * 16 + z_at) * 4 + x_at)
+                    groups.append(group)
+    return groups
+
+
+def gather(block, axes, count, groups=None):
     copies = jnp.broadcast_to(block[None], (count,) + block.shape)
-    return lax.all_to_all(copies, axes, 0, 0, tiled=True)
+    return lax.all_to_all(copies, axes, 0, 0, axis_index_groups=groups, tiled=True)
 
 
 def body(tokens, gain, key_cotangent, global_params, local_params, momentum, sign_bits):
     sign_vec = (2 * sign_bits - 1).astype(jnp.float32)
-    drift = global_params - local_params[0].astype(jnp.float32)
-    row_count, width = drift.shape
-    terms = clip_terms(rotate(drift, sign_vec)).reshape(row_count, width).astype(jnp.bfloat16)
-    all_terms = gather(terms, REPLICA)
-    replicas = all_terms.shape[0]
-    summed = jnp.sum(all_terms.astype(jnp.float32), axis=0)
+    all_local = gather(local_params[0], REPLICA, 4)
+    drift = global_params[None] - all_local.astype(jnp.float32)
+    replicas, row_count, width = drift.shape
+    terms = clip_terms(rotate(drift, sign_vec)).reshape(replicas, row_count, width).astype(jnp.bfloat16)
+    summed = jnp.sum(terms.astype(jnp.float32), axis=0)
     new_params, new_momentum = outer_update(global_params, momentum, summed / replicas, sign_vec)
     weight_part = new_params.astype(jnp.bfloat16)
 
     half = width // 2
     core = lax.axis_index("core")
     mine = jnp.where(core == 0, weight_part[:, :half], weight_part[:, half:])
-    got = gather(mine, ("y1", "zh"))
-    got = gather(got, ("y0", "z0", "x"))
-    got = got.reshape(2, 2, 4, 2, 8, row_count, half).transpose(3, 0, 4, 1, 2, 5, 6)
+    got = gather(mine, ("y1", "zh", "x1"), 32)
+    got = gather(got, AXES, 8, cubes())
+    got = got.reshape(2, 2, 2, 2, 8, 2, row_count, half).transpose(3, 0, 4, 1, 5, 2, 6, 7)
     got = got.reshape(-1, half)
     other = lax.ppermute(got, "core", [(0, 1), (1, 0)])
-    low = jnp.where(core == 0, got, other)
-    high = jnp.where(core == 0, other, got)
-    weight = jnp.concatenate([low, high], axis=1)
 
     tok_float = tokens[0].astype(jnp.float32)
     gain_vec = gain[0]
-    cotangent = key_cotangent[0]
     inverse = lax.rsqrt(jnp.mean(tok_float * tok_float, axis=-1, keepdims=True) + NORM_EPS)
     normed = tok_float * inverse
     hidden = (normed * gain_vec).astype(jnp.bfloat16)
-    keys = jnp.dot(hidden, weight, preferred_element_type=jnp.float32)
-    back = lax.dot_general(cotangent, weight, (((1,), (1,)), ((), ())), preferred_element_type=jnp.float32)
-    scaled = back * gain_vec
+    low, high = key_cotangent[0][:, :half], key_cotangent[0][:, half:]
+
+    def both(cotangent, weight):
+        keys = jnp.dot(hidden, weight, preferred_element_type=jnp.float32)
+        back = lax.dot_general(cotangent, weight, (((1,), (1,)), ((), ())), preferred_element_type=jnp.float32)
+        return keys.astype(jnp.bfloat16), back
+
+    keys_mine, back_mine = both(jnp.where(core == 0, low, high), got)
+    keys_other, back_other = both(jnp.where(core == 0, high, low), other)
+    key_low = jnp.where(core == 0, keys_mine, keys_other)
+    key_high = jnp.where(core == 0, keys_other, keys_mine)
+    keys = jnp.concatenate([key_low, key_high], axis=1)
+    scaled = (back_mine + back_other) * gain_vec
     centre = jnp.mean(scaled * normed, axis=-1, keepdims=True)
     grads = (inverse * (scaled - normed * centre)).astype(jnp.bfloat16)
-    key_out = keys.astype(jnp.bfloat16)[None]
-    grad_tokens = grads[None]
-    return (key_out, grad_tokens, new_params, new_momentum)
+    return (keys[None], grads[None], new_params, new_momentum)
 
 
 def solution(mesh):

time: 101 us -> 101 us (level)
  blocking collectives: 55.2 us -> 58.9 us
  starting transfers between devices: 22.7 us -> 19.5 us
  waiting for transfers between devices: 10.5 us -> 8.41 us
  local copies, waits for them, and re-layouts: 1.1 us -> 2.13 us
    all_to_all x2, blocking collectives: 55.2 us -> 58.9 us  [gather(): lax.all_to_all(copies, axes, 0, 0, axis_index_groups=groups, tiled=True)]
    ppermute x1, starting transfers between devices: 5.27 us -> 2.05 us  [body(): other = lax.ppermute(got, 'core', [(0, 1), (1, 0)])]
    ppermute x1, waiting for transfers between devices: 3.34 us -> 1.93 us  [body(): other = lax.ppermute(got, 'core', [(0, 1), (1, 0)])]
    broadcast_in_dim x1 -> x2, other arithmetic: 1.97 us -> 2.6 us  [body(): return (keys[None], grads[None], new_params, new_momentum)]
    dot_general x2 -> x4, matrix products: 3.36 us -> 3.15 us  [the longest x2 1.89 us: both(): lax.dot_general(cotangent, weight, (((1,), (1,)), ((), ())), preferred_el...]
  transfers between devices with their start and end apart: 2 -> 2, of which waited for: 2 -> 2; matrix products, arithmetic and copies ran while one was open for 0% -> 3% of each run, Pallas kernels for 0% -> 0%
where the time goes in v3:
time: 101 us; the launch traced here: 100 us
  blocking collectives  58.9 us (58%)
  starting transfers between devices  19.5 us (19%)
  waiting for transfers between devices  8.41 us (8%)
  matrix products  5.37 us (5%)
  other arithmetic  5.22 us (5%)
  local copies, waits for them, and re-layouts  2.13 us (2%)
    all_to_all x2, blocking collectives, gather(): lax.all_to_all(copies, axes, 0, 0, axis_index_groups=groups, tiled=True)  58.9 us
    all_to_all x1, starting transfers between devices, gather(): lax.all_to_all(copies, axes, 0, 0, axis_index_groups=groups, tiled=True)  17.4 us
    all_to_all x1, waiting for transfers between devices, gather(): lax.all_to_all(copies, axes, 0, 0, axis_index_groups=groups, tiled=True)  6.48 us
    broadcast_in_dim x2, other arithmetic, body(): return (keys[None], grads[None], new_params, new_momentum)  2.6 us
    ppermute x1, starting transfers between devices, body(): other = lax.ppermute(got, 'core', [(0, 1), (1, 0)])  2.05 us
  transfers between devices with their start and end apart: 2, of which 2 were waited for; matrix products, arithmetic and copies ran while one was open for 3% of the time, Pallas kernels for 0%

profile of v3, /device:TPU:1, one launch (start us, length us, event | category | flops | bytes accessed | tf_op | source)
XLA Modules:
  0.0 100.2 jit_solution(9954915555004251009)
XLA Ops:
  0.6 1.4 %broadcast_in_dim.13 = bf16[4,16,512]{2,1,0:T(8,128)(2,1)} broadcast(bf16[16,512]{1,0:T(8,128)(2,1)} %bitcast.85), dimensions={1,2} | broadcast | bytes 81920 | tf_op jit(solution)/shard_map/broadcast_in_dim | solution.py:71
  2.0 17.4 %all-to-all-start = ((bf16[4,16,512]{2,1,0:T(8,128)(2,1)}), bf16[4,16,512]{2,1,0:T(8,128)(2,1)S(1)}, u32[]{:S(2)}, u32[]{:S(2)}) async-start(bf16[4,16,512]{2,1,0:T(8,128)(2,1)} %broadcast_in_dim.13), calls=%async_computation | async-start | bytes 131072 | tf_op jit(solution)/shard_map/all_to_all | solution.py:72
  19.4 0.7 add_convert_fusion
  20.1 6.5 %all-to-all-done = bf16[4,16,512]{2,1,0:T(8,128)(2,1)S(1)} async-done(((bf16[4,16,512]{2,1,0:T(8,128)(2,1)}), bf16[4,16,512]{2,1,0:T(8,128)(2,1)S(1)}, u32[]{:S(2)}, u32[]{:S(2)}) %all-to-all-start) | async-done | bytes 65568 | tf_op jit(solution)/shard_map/all_to_all | solution.py:72
  26.6 1.2 %abs_reduce_fusion = (f32[4,16,4]{1,2,0:T(4,128)S(1)}, f32[4,16,4,128]{3,1,2,0:T(8,128)S(1)}) fusion(f32[128,128,1,1]{1,0,3,2:T(8,128)} %constant.45, bf16[4,16,512]{2,1,0:T(8,128)(2,1)S(1)} %all-to-all-done, f32[512]{0:T(512)S(1)} %add_convert_fusion, f32[16,512]{1,0:T(8,128)} %param.12), kind=kOutput, calls=%fused_computation.34 | convolution fusion | flops 50495232 | bytes 297984 | tf_op jit(solution)/shard_map/...bi,ij->...bj/dot_general | solution.py:37
  27.8 0.1 convert_reduce_fusion
  27.9 1.0 %convolution_bitcast_fusion = f32[4,2,8,128]{3,2,1,0:T(8,128)S(1)} fusion(f32[128,128,1]{1,0,2:T(8,128)} %constant.46, f32[16,4,128]{2,0,1:T(8,128)S(1)} %convert_reduce_fusion), kind=kOutput, calls=%fused_computation.27 | convolution fusion | flops 12591104 | bytes 131072 | tf_op jit(solution)/shard_map/rbi,ij->rbj/dot_general | solution.py:48
  28.9 1.4 %fusion.45 = (bf16[16,512]{1,0:T(8,128)(2,1)S(1)}, f32[16,512]{1,0:T(8,128)}, f32[16,512]{1,0:T(8,128)}) fusion(f32[16,512]{1,0:T(8,128)} %param.12, f32[512]{0:T(512)S(1)} %add_convert_fusion, f32[4,2,8,128]{3,2,1,0:T(8,128)S(1)} %convolution_bitcast_fusion, f32[16,512]{1,0:T(8,128)} %param.14), kind=kLoop, calls=%fused_computation.58 | loop fusion | flops 65536 | bytes 182272 | tf_op jit(solution)/shard_map/convert_element_type | solution.py:83
  30.4 31.9 %all_to_all.15 = bf16[32,16,256]{2,1,0:T(8,128)(2,1)S(1)} all-to-all(bf16[32,16,256]{2,1,0:T(8,128)(2,1)S(1)} %broadcast_in_dim.14), channel_id=1, replica_groups=mesh['yh'=2,'core'=2,'y1'=2,'y0'=2,'zh'=8,'z0'=2,'x1'=2,'x0'=2] {'y1','z..., dimensions={0} | all-to-all | bytes 524288 | tf_op jit(solution)/shard_map/all_to_all | solution.py:72
  62.3 0.2 broadcast_in_dim.15
  62.5 27.0 %all_to_all.16 = bf16[8,32,16,256]{3,2,1,0:T(8,128)(2,1)S(1)} all-to-all(bf16[8,32,16,256]{3,2,1,0:T(8,128)(2,1)S(1)} %broadcast_in_dim.15), channel_id=1, replica_groups={{0,1,4,5,64,65,68,69},{2,3,6,7,66,67,70,71},{8,9,12,13,72,73,76,77},{10..., dimensions={0} | all-to-all | bytes 4194304 | tf_op jit(solution)/shard_map/all_to_all | solution.py:72
  89.4 0.0 copy-start
  89.4 0.0 copy-start.2
  89.4 0.3 copy.17
  89.7 2.1 %collective-permute-start = (bf16[4096,256]{1,0:T(8,128)(2,1)S(1)}, bf16[4096,256]{1,0:T(8,128)(2,1)S(1)}, u32[]{:S(2)}, u32[]{:S(2)}) collective-permute-start(bf16[4096,256]{1,0:T(8,128)(2,1)S(1)} %bitcast.76), channel_id=1, source_target_pairs={{0,256},{256,0},{1,257},{257,1},{2,258},{258,2},{3,259},{259,3},{4... | collective-permute-start | bytes 6291464 | tf_op jit(solution)/shard_map/ppermute | solution.py:92
  91.8 0.0 copy-done
  91.8 0.4 fusion.11
  92.2 0.0 copy-done.2
  92.2 0.0 copy-start.1
  92.2 0.6 fusion.27
  92.9 0.3 copy-done.1
  93.2 0.8 fusion.34
  94.0 1.9 %collective-permute-done = bf16[4096,256]{1,0:T(8,128)(2,1)S(1)} collective-permute-done((bf16[4096,256]{1,0:T(8,128)(2,1)S(1)}, bf16[4096,256]{1,0:T(8,128)(2,1)S(1)}, u32[]{:S(2)}, u32[]{:S(2)}) %collective-permute-start) | collective-permute-done | bytes 2097184 | tf_op jit(solution)/shard_map/ppermute | solution.py:92
  95.9 1.0 %fusion.7 = (f32[192]{0:T(256)S(1)}, f32[192,4096]{1,0:T(8,128)S(1)}) fusion(bf16[1,192,4096]{2,1,0:T(8,128)(2,1)S(1)} %copy-done, f32[192]{0:T(256)S(1)} %add_rsqrt_fusion, f32[4096]{0:T(1024)S(1)} %bitcast.83, f32[192,4096]{1,0:T(8,128)S(1)} %fusion.34, bf16[4096,256]{1,0:T(8,128)(2,1)S(1)} %collective-permute-done, pred[]{:T(512)S(6)} %eq.2, ...), kind=kOutput, calls=%fused_computation.10 | convolution fusion | flops 407420736 | bytes 10176001 | tf_op jit(solution)/shard_map/dot_general | solution.py:103
  97.0 0.6 broadcast_select_fusion.1
  97.6 0.7 maximum_bitcast_fusion
  98.3 1.9 %fusion.17 = bf16[1,192,4096]{2,1,0:T(8,128)(2,1)} fusion(f32[192,4096]{1,0:T(8,128)S(1)} %get-tuple-element.12, bf16[1,192,4096]{2,1,0:T(8,128)(2,1)S(1)} %copy-done, f32[192]{0:T(256)S(1)} %broadcast_multiply_fusion, f32[192]{0:T(256)S(1)} %add_rsqrt_fusion), kind=kLoop, calls=%fused_computation.19 | loop fusion | flops 4718592 | bytes 6292992 | tf_op jit(solution)/shard_map/broadcast_in_dim | solution.py:114
  (5 shorter events, 0.0 us)
Async XLA Ops:
  2.0 24.6 %all-to-all-start = ((bf16[4,16,512]{2,1,0:T(8,128)(2,1)}), bf16[4,16,512]{2,1,0:T(8,128)(2,1)S(1)}, u32[]{:S(2)}, u32[]{:S(2)}) async-start(bf16[4,16,512]{2,1,0:T(8,128)(2,1)} %broadcast_in_dim.13), calls=%async_computation | async-start | bytes 131072 | tf_op jit(solution)/shard_map/all_to_all | solution.py:72
  89.4 2.4 %copy-start = (bf16[1,192,4096]{2,1,0:T(8,128)(2,1)S(1)}, bf16[1,192,4096]{2,1,0:T(8,128)(2,1)}, u32[]{:S(2)}) copy-start(bf16[1,192,4096]{2,1,0:T(8,128)(2,1)} %param.9) | copy-start | bytes 4718596
  89.4 2.8 %copy-start.2 = (f32[1,4096]{1,0:T(1,128)S(1)}, f32[1,4096]{1,0:T(1,128)}, u32[]{:S(2)}) copy-start(f32[1,4096]{1,0:T(1,128)} %param.10) | copy-start | bytes 49156
  89.7 6.2 %collective-permute-start = (bf16[4096,256]{1,0:T(8,128)(2,1)S(1)}, bf16[4096,256]{1,0:T(8,128)(2,1)S(1)}, u32[]{:S(2)}, u32[]{:S(2)}) collective-permute-start(bf16[4096,256]{1,0:T(8,128)(2,1)S(1)} %bitcast.76), channel_id=1, source_target_pairs={{0,256},{256,0},{1,257},{257,1},{2,258},{258,2},{3,259},{259,3},{4... | collective-permute-start | bytes 6291464 | tf_op jit(solution)/shard_map/ppermute | solution.py:92
  92.2 0.9 copy-start.1

commit v4 on v3

--- a/solution.py
+++ b/solution.py
@@ -4,6 +4,8 @@
 import jax.numpy as jnp
 import numpy as np
 from jax import lax
+from jax.experimental import pallas as pl
+from jax.experimental.pallas import tpu as pltpu
 from jax.sharding import Mesh, PartitionSpec as P
 
 HB = 128
@@ -20,36 +22,65 @@
 AXES = tuple(SIZES)
 
 
-def hadamard(order):
-    counter = np.arange(order)
-    common = counter[:, None] & counter[None, :]
-    parity = common & 0
-    shift = 0
-    while 1 << shift < order:
-        parity = parity ^ common >> shift & 1
-        shift = shift + 1
-    return jnp.asarray((1 - 2 * parity) / math.sqrt(order), dtype=jnp.float32)
+def signs():
+    common = lax.broadcasted_iota(jnp.int32, (HB, HB), 0) & lax.broadcasted_iota(jnp.int32, (HB, HB), 1)
+    for shift in (4, 2, 1):
+        common = common ^ (common >> shift)
+    return (1 - 2 * (common & 1)).astype(jnp.float32).astype(jnp.bfloat16)
 
 
-def rotate(values, sign_vec):
-    width = values.shape[-1]
-    blocks = (values * sign_vec).reshape(values.shape[:-1] + (width // HB, HB))
-    return jnp.einsum("...bi,ij->...bj", blocks, hadamard(HB), precision=lax.Precision.HIGHEST)
+def rotate(values, matrix):
+    total = None
+    rest = values
+    for _ in range(3):
+        part = rest.astype(jnp.bfloat16)
+        rest = rest - part.astype(jnp.float32)
+        product = jnp.dot(part, matrix, preferred_element_type=jnp.float32)
+        total = product if total is None else total + product
+    return total * (1.0 / math.sqrt(HB))
 
 
-def clip_terms(rotated):
+def update_kernel(local_ref, global_ref, moment_ref, bits_ref, weight_ref, params_ref, fresh_ref):
+    replicas, row_count, width = local_ref.shape
+    count = width // HB
+    matrix = signs()
+    sign_vec = (2 * bits_ref[...] - 1).astype(jnp.float32)
+    global_rows = global_ref[...]
+    pieces = []
+    for replica in range(replicas):
+        drift = (global_rows - local_ref[replica].astype(jnp.float32)) * sign_vec
+        pieces += [drift[:, at * HB : (at + 1) * HB] for at in range(count)]
+    rotated = rotate(jnp.concatenate(pieces, axis=0), matrix)
     block_scale = jnp.mean(jnp.abs(rotated), axis=-1, keepdims=True) + NORM_EPS
-    return jnp.clip(rotated / block_scale, -CLIP_LEVEL, CLIP_LEVEL) * block_scale
+    terms = jnp.clip(rotated / block_scale, -CLIP_LEVEL, CLIP_LEVEL) * block_scale
+    terms = terms.astype(jnp.bfloat16).astype(jnp.float32)
+    rows = count * row_count
+    summed = terms[:rows]
+    for replica in range(1, replicas):
+        summed = summed + terms[replica * rows : (replica + 1) * rows]
+    restored = rotate(summed / replicas, matrix)
+    restored = jnp.concatenate([restored[at * row_count : (at + 1) * row_count] for at in range(count)], axis=1)
+    pseudo = restored * sign_vec
+    fresh = OUTER_MU * moment_ref[...] + pseudo
+    params = global_rows - OUTER_LR * (pseudo + OUTER_MU * fresh)
+    fresh_ref[...] = fresh
+    params_ref[...] = params
+    weight_ref[...] = params.astype(jnp.bfloat16)
 
 
-def outer_update(global_rows, moment_rows, averaged, sign_vec):
-    row_count, width = global_rows.shape
-    blocks = averaged.reshape(row_count, width // HB, HB)
-    restored = jnp.einsum("rbi,ij->rbj", blocks, hadamard(HB), precision=lax.Precision.HIGHEST)
-    pseudo = restored.reshape(row_count, width) * sign_vec
-    fresh_moment = OUTER_MU * moment_rows + pseudo
-    fresh_params = global_rows - OUTER_LR * (pseudo + OUTER_MU * fresh_moment)
-    return (fresh_params, fresh_moment)
+def outer_update(all_local, global_params, momentum, sign_bits):
+    row_count, width = global_params.shape
+    return pl.pallas_call(
+        update_kernel,
+        out_shape=(
+            jax.ShapeDtypeStruct((row_count, width), jnp.bfloat16),
+            jax.ShapeDtypeStruct((row_count, width), jnp.float32),
+            jax.ShapeDtypeStruct((row_count, width), jnp.float32),
+        ),
+        in_specs=[pl.BlockSpec(memory_space=pltpu.VMEM)] * 4,
+        out_specs=[pl.BlockSpec(memory_space=pltpu.VMEM)] * 3,
+        cost_estimate=pl.CostEstimate(flops=20_000_000, bytes_accessed=250_000, transcendentals=0),
+    )(all_local, global_params, momentum, sign_bits.reshape(1, width))
 
 
 def cubes():
@@ -73,21 +104,17 @@
 
 
 def body(tokens, gain, key_cotangent, global_params, local_params, momentum, sign_bits):
-    sign_vec = (2 * sign_bits - 1).astype(jnp.float32)
     all_local = gather(local_params[0], REPLICA, 4)
-    drift = global_params[None] - all_local.astype(jnp.float32)
-    replicas, row_count, width = drift.shape
-    terms = clip_terms(rotate(drift, sign_vec)).reshape(replicas, row_count, width).astype(jnp.bfloat16)
-    summed = jnp.sum(terms.astype(jnp.float32), axis=0)
-    new_params, new_momentum = outer_update(global_params, momentum, summed / replicas, sign_vec)
-    weight_part = new_params.astype(jnp.bfloat16)
+    weight_part, new_params, new_momentum = outer_update(all_local, global_params, momentum, sign_bits)
+    row_count, width = global_params.shape
 
     half = width // 2
     core = lax.axis_index("core")
     mine = jnp.where(core == 0, weight_part[:, :half], weight_part[:, half:])
-    got = gather(mine, ("y1", "zh", "x1"), 32)
+    got = gather(mine, ("zh",), 8)
+    got = gather(got, ("y1", "x1"), 4)
     got = gather(got, AXES, 8, cubes())
-    got = got.reshape(2, 2, 2, 2, 8, 2, row_count, half).transpose(3, 0, 4, 1, 5, 2, 6, 7)
+    got = got.reshape(2, 2, 2, 2, 2, 8, row_count, half).transpose(3, 0, 5, 1, 4, 2, 6, 7)
     got = got.reshape(-1, half)
     other = lax.ppermute(got, "core", [(0, 1), (1, 0)])
 
@@ -105,9 +132,9 @@
 
     keys_mine, back_mine = both(jnp.where(core == 0, low, high), got)
     keys_other, back_other = both(jnp.where(core == 0, high, low), other)
-    key_low = jnp.where(core == 0, keys_mine, keys_other)
-    key_high = jnp.where(core == 0, keys_other, keys_mine)
-    keys = jnp.concatenate([key_low, key_high], axis=1)
+    keys = jnp.zeros((keys_mine.shape[0], width), jnp.bfloat16)
+    keys = lax.dynamic_update_slice(keys, keys_mine, (0, core * half))
+    keys = lax.dynamic_update_slice(keys, keys_other, (0, half - core * half))
     scaled = (back_mine + back_other) * gain_vec
     centre = jnp.mean(scaled * normed, axis=-1, keepdims=True)
     grads = (inverse * (scaled - normed * centre)).astype(jnp.bfloat16)

time: 101 us -> 105 us (1.040)
  matrix products: 5.37 us -> 9.55 us
  blocking collectives: 58.9 us -> 56.2 us
  local copies, waits for them, and re-layouts: 2.13 us -> 4.59 us
  other arithmetic: 5.22 us -> 3.04 us
  Pallas kernels: 0 us -> 1.99 us
  waiting for transfers between devices: 8.41 us -> 7.17 us
  starting transfers between devices: 19.5 us -> 20.7 us
    dot_general x2, matrix products: 1.27 us -> 4.47 us  [both(): keys = jnp.dot(hidden, weight, preferred_element_type=jnp.float32)]
    dot_general x2, matrix products: 1.89 us -> 5.08 us  [both(): lax.dot_general(cotangent, weight, (((1,), (1,)), ((), ())), preferred_el...]
    all_to_all x2 -> x3, blocking collectives: 58.9 us -> 56.2 us  [gather(): lax.all_to_all(copies, axes, 0, 0, axis_index_groups=groups, tiled=True)]
    dot_general x2 -> x0, matrix products: 2.22 us -> none  [the longest x1 1.2 us: rotate(): jnp.einsum('...bi,ij->...bj', blocks, hadamard(HB), precision=lax.Precisi...]
    convert_element_type x2 -> x0, other arithmetic: 2.1 us -> none  [the longest x1 1.41 us: body(): weight_part = new_params.astype(jnp.bfloat16)]
    pallas_call x0 -> x1, Pallas kernels: none -> 1.99 us  [outer_update(): pl.pallas_call(update_kernel, out_shape=(jax.ShapeDtypeStruct((row_count,...]
    ppermute x1, waiting for transfers between devices: 1.93 us -> 0.01 us  [body(): other = lax.ppermute(got, 'core', [(0, 1), (1, 0)])]
    transpose x1, local copies, waits for them, and re-layouts: 0.29 us -> 1.65 us  [body(): got.reshape(2, 2, 2, 2, 2, 8, row_count, half)]
  transfers between devices with their start and end apart: 2 -> 2, of which waited for: 2 -> 1; matrix products, arithmetic and copies ran while one was open for 3% -> 5% of each run, Pallas kernels for 0% -> 0%
where the time goes in v4:
time: 105 us; the launch traced here: 104 us
  blocking collectives  56.2 us (54%)
  starting transfers between devices  20.7 us (20%)
  matrix products  9.55 us (9%)
  waiting for transfers between devices  7.17 us (7%)
  local copies, waits for them, and re-layouts  4.59 us (4%)
  other arithmetic  3.04 us (3%)
  Pallas kernels  1.99 us (2%)
    all_to_all x3, blocking collectives, gather(): lax.all_to_all(copies, axes, 0, 0, axis_index_groups=groups, tiled=True)  56.2 us
    all_to_all x1, starting transfers between devices, gather(): lax.all_to_all(copies, axes, 0, 0, axis_index_groups=groups, tiled=True)  17.4 us
    all_to_all x1, waiting for transfers between devices, gather(): lax.all_to_all(copies, axes, 0, 0, axis_index_groups=groups, tiled=True)  7.17 us
    dot_general x2, matrix products, both(): lax.dot_general(cotangent, weight, (((1,), (1,)), ((), ())), preferred_el...  5.08 us
    dot_general x2, matrix products, both(): keys = jnp.dot(hidden, weight, preferred_element_type=jnp.float32)  4.47 us
    ppermute x1, starting transfers between devices, body(): other = lax.ppermute(got, 'core', [(0, 1), (1, 0)])  3.31 us
  transfers between devices with their start and end apart: 2, of which 1 were waited for; matrix products, arithmetic and copies ran while one was open for 5% of the time, Pallas kernels for 0%

profile of v4, /device:TPU:1, one launch (start us, length us, event | category | flops | bytes accessed | tf_op | source)
XLA Modules:
  0.0 104.0 jit_solution(11972869096091165730)
XLA Ops:
  0.6 1.4 %broadcast_in_dim.40 = bf16[4,16,512]{2,1,0:T(8,128)(2,1)} broadcast(bf16[16,512]{1,0:T(8,128)(2,1)} %bitcast.70), dimensions={1,2} | broadcast | bytes 81920 | tf_op jit(solution)/shard_map/broadcast_in_dim | solution.py:102
  2.0 17.4 %all-to-all-start = ((bf16[4,16,512]{2,1,0:T(8,128)(2,1)}), bf16[4,16,512]{2,1,0:T(8,128)(2,1)S(1)}, u32[]{:S(2)}, u32[]{:S(2)}) async-start(bf16[4,16,512]{2,1,0:T(8,128)(2,1)} %broadcast_in_dim.40), calls=%async_computation | async-start | bytes 131072 | tf_op jit(solution)/shard_map/all_to_all | solution.py:103
  19.4 7.2 %all-to-all-done.local_ref = bf16[4,16,512]{2,1,0:T(8,128)(2,1)S(1)} async-done(((bf16[4,16,512]{2,1,0:T(8,128)(2,1)}), bf16[4,16,512]{2,1,0:T(8,128)(2,1)S(1)}, u32[]{:S(2)}, u32[]{:S(2)}) %all-to-all-start) | async-done | bytes 65568 | tf_op jit(solution)/shard_map/all_to_all | solution.py:103
  26.6 0.0 copy-start.1
  26.6 0.6 copy-done.1
  27.2 2.0 %shard_map.102 = (bf16[16,512]{1,0:T(8,128)(2,1)}, f32[16,512]{1,0:T(8,128)}, f32[16,512]{1,0:T(8,128)}) custom-call(bf16[4,16,512]{2,1,0:T(8,128)(2,1)} %copy-done.1, f32[16,512]{1,0:T(8,128)} %global_ref.1, f32[16,512]{1,0:T(8,128)} %moment_ref.1, s32[1,512]{1,0:T(1,128)} %bitcast.71), custom_call_target="tpu_custom_call" | custom-call | flops 20000000 | bytes 250000 | tf_op jit(solution)/shard_map/pallas_call | solution.py:73
  29.2 0.7 slice_select_fusion
  29.9 21.9 %all_to_all.20 = bf16[8,16,256]{2,1,0:T(8,128)(2,1)S(1)} all-to-all(bf16[8,16,256]{2,1,0:T(8,128)(2,1)S(1)} %broadcast_in_dim.41), channel_id=1, replica_groups=mesh['yh'=2,'core'=2,'y1'=2,'y0'=2,'zh'=8,'z0'=2,'x1'=2,'x0'=2] {'zh'}, dimensions={0} | all-to-all | bytes 131072 | tf_op jit(solution)/shard_map/all_to_all | solution.py:103
  51.9 12.5 %all_to_all.21 = bf16[4,8,16,256]{3,2,1,0:T(8,128)(2,1)S(1)} all-to-all(bf16[4,8,16,256]{3,2,1,0:T(8,128)(2,1)S(1)} %broadcast_in_dim.42), channel_id=1, replica_groups=mesh['yh'=2,'core'=2,'y1'=2,'y0'=2,'zh'=8,'z0'=2,'x1'=2,'x0'=2] {'y1','x1'}, dimensions={0} | all-to-all | bytes 524288 | tf_op jit(solution)/shard_map/all_to_all | solution.py:103
  64.4 0.2 broadcast_in_dim.43
  64.6 21.7 %all_to_all.22 = bf16[8,4,8,16,256]{4,3,2,1,0:T(8,128)(2,1)S(1)} all-to-all(bf16[8,4,8,16,256]{4,3,2,1,0:T(8,128)(2,1)S(1)} %broadcast_in_dim.43), channel_id=1, replica_groups={{0,1,4,5,64,65,68,69},{2,3,6,7,66,67,70,71},{8,9,12,13,72,73,76,77},{10..., dimensions={0} | all-to-all | bytes 4194304 | tf_op jit(solution)/shard_map/all_to_all | solution.py:103
  86.3 0.0 copy-start
  86.3 0.0 copy-start.4
  86.3 1.7 %copy.11 = bf16[2,2,8,2,2,2,16,256]{7,6,5,4,3,2,1,0:T(8,128)(2,1)} copy(bf16[2,2,8,2,2,2,16,256]{7,6,2,4,0,5,3,1:T(8,128)(2,1)S(1)} %bitcast.64) | data formatting | bytes 4194304 | tf_op jit(solution)/shard_map/transpose | solution.py:117
  88.0 3.3 %collective-permute-start = (bf16[4096,256]{1,0:T(8,128)(2,1)}, bf16[4096,256]{1,0:T(8,128)(2,1)}, u32[]{:S(2)}, u32[]{:S(2)}) collective-permute-start(bf16[4096,256]{1,0:T(8,128)(2,1)} %bitcast.7), channel_id=1, source_target_pairs={{0,256},{256,0},{1,257},{257,1},{2,258},{258,2},{3,259},{259,3},{4... | collective-permute-start | bytes 6291464 | tf_op jit(solution)/shard_map/ppermute | solution.py:119
  91.3 0.0 copy-done
  91.3 0.4 fusion.11
  91.8 0.0 copy-done.4
  91.8 0.0 copy-start.2
  91.8 2.3 %fusion.33 = bf16[1,192,512]{2,1,0:T(8,128)(2,1)S(1)} fusion(bf16[1,192,512]{2,1,0:T(8,128)(2,1)S(1)} %broadcast_in_dim.18, s32[]{:T(128)S(6)} %select_n.28, bf16[4096,256]{1,0:T(8,128)(2,1)} %bitcast.7, bf16[1,192,4096]{2,1,0:T(8,128)(2,1)S(1)} %copy-done, f32[4096]{0:T(1024)S(1)} %bitcast.67, f32[192]{0:T(256)S(1)} %add_rsqrt_fusion), kind=kOutput, calls=%fused_computation.28 | convolution fusion | flops 405848064 | bytes 3785732 | tf_op jit(solution)/shard_map/dot_general | solution.py:129
  94.0 0.0 copy-done.2
  94.1 2.4 %fusion.43 = f32[192,4096]{1,0:T(8,128)S(1)} fusion(bf16[4096,256]{1,0:T(8,128)(2,1)} %bitcast.7, pred[]{:T(512)S(6)} %eq.2, bf16[192,512]{1,0:T(8,128)(2,1)S(1)} %bitcast.65), kind=kOutput, calls=%fused_computation.32 | convolution fusion | flops 402702336 | bytes 5439489 | tf_op jit(solution)/shard_map/dot_general | solution.py:130
  96.5 0.0 collective-permute-done
  96.5 2.6 %fusion.7 = (f32[192]{0:T(256)S(1)}, f32[192,4096]{1,0:T(8,128)S(1)}) fusion(bf16[1,192,4096]{2,1,0:T(8,128)(2,1)S(1)} %copy-done, f32[192]{0:T(256)S(1)} %add_rsqrt_fusion, f32[4096]{0:T(1024)S(1)} %bitcast.68, f32[192,4096]{1,0:T(8,128)S(1)} %fusion.43, bf16[4096,256]{1,0:T(8,128)(2,1)} %collective-permute-done, pred[]{:T(512)S(6)} %eq.2, ...), kind=kOutput, calls=%fused_computation.10 | convolution fusion | flops 407420736 | bytes 10176001 | tf_op jit(solution)/shard_map/dot_general | solution.py:130
  99.2 1.9 %fusion.17 = bf16[1,192,4096]{2,1,0:T(8,128)(2,1)} fusion(f32[192,4096]{1,0:T(8,128)S(1)} %get-tuple-element.11, bf16[1,192,4096]{2,1,0:T(8,128)(2,1)S(1)} %copy-done, f32[192]{0:T(256)S(1)} %broadcast_multiply_fusion, f32[192]{0:T(256)S(1)} %add_rsqrt_fusion), kind=kLoop, calls=%fused_computation.19 | loop fusion | flops 4718592 | bytes 6292992 | tf_op jit(solution)/shard_map/broadcast_in_dim | solution.py:141
  101.1 2.2 %fusion.39 = bf16[1,192,512]{2,1,0:T(8,128)(2,1)S(1)} fusion(bf16[1,192,512]{2,1,0:T(8,128)(2,1)S(1)} %fusion.33, s32[]{:T(128)S(6)} %select_n.29, bf16[4096,256]{1,0:T(8,128)(2,1)} %collective-permute-done, bf16[1,192,4096]{2,1,0:T(8,128)(2,1)S(1)} %copy-done, f32[4096]{0:T(1024)S(1)} %bitcast.69, f32[192]{0:T(256)S(1)} %add_rsqrt_fusion), kind=kOutput, calls=%fused_computation.30 | convolution fusion | flops 405848064 | bytes 3785732 | tf_op jit(solution)/shard_map/dot_general | solution.py:129
  103.3 0.0 copy-start.3
  103.3 0.7 copy-done.3
  (5 shorter events, 0.1 us)
Async XLA Ops:
  2.0 24.6 %all-to-all-start = ((bf16[4,16,512]{2,1,0:T(8,128)(2,1)}), bf16[4,16,512]{2,1,0:T(8,128)(2,1)S(1)}, u32[]{:S(2)}, u32[]{:S(2)}) async-start(bf16[4,16,512]{2,1,0:T(8,128)(2,1)} %broadcast_in_dim.40), calls=%async_computation | async-start | bytes 131072 | tf_op jit(solution)/shard_map/all_to_all | solution.py:103
  26.6 0.6 copy-start.1
  86.3 5.0 %copy-start = (bf16[1,192,4096]{2,1,0:T(8,128)(2,1)S(1)}, bf16[1,192,4096]{2,1,0:T(8,128)(2,1)}, u32[]{:S(2)}) copy-start(bf16[1,192,4096]{2,1,0:T(8,128)(2,1)} %param.7) | copy-start | bytes 4718596
  86.3 5.4 %copy-start.4 = (f32[1,4096]{1,0:T(1,128)S(1)}, f32[1,4096]{1,0:T(1,128)}, u32[]{:S(2)}) copy-start(f32[1,4096]{1,0:T(1,128)} %param.8) | copy-start | bytes 49156
  88.0 8.5 %collective-permute-start = (bf16[4096,256]{1,0:T(8,128)(2,1)}, bf16[4096,256]{1,0:T(8,128)(2,1)}, u32[]{:S(2)}, u32[]{:S(2)}) collective-permute-start(bf16[4096,256]{1,0:T(8,128)(2,1)} %bitcast.7), channel_id=1, source_target_pairs={{0,256},{256,0},{1,257},{257,1},{2,258},{258,2},{3,259},{259,3},{4... | collective-permute-start | bytes 6291464 | tf_op jit(solution)/shard_map/ppermute | solution.py:119
  91.8 2.3 %copy-start.2 = (bf16[1,192,512]{2,1,0:T(8,128)(2,1)S(1)}, bf16[1,192,512]{2,1,0:T(8,128)(2,1)}, u32[]{:S(2)}) copy-start(bf16[1,192,512]{2,1,0:T(8,128)(2,1)} %param.9) | copy-start | bytes 589828
  103.3 0.7 copy-start.3

commit v5 on v4

--- a/solution.py
+++ b/solution.py
@@ -40,7 +40,7 @@
     return total * (1.0 / math.sqrt(HB))
 
 
-def update_kernel(local_ref, global_ref, moment_ref, bits_ref, weight_ref, params_ref, fresh_ref):
+def update_kernel(local_ref, global_ref, moment_ref, bits_ref, weight_ref, pseudo_ref):
     replicas, row_count, width = local_ref.shape
     count = width // HB
     matrix = signs()
@@ -61,11 +61,15 @@
     restored = rotate(summed / replicas, matrix)
     restored = jnp.concatenate([restored[at * row_count : (at + 1) * row_count] for at in range(count)], axis=1)
     pseudo = restored * sign_vec
-    fresh = OUTER_MU * moment_ref[...] + pseudo
-    params = global_rows - OUTER_LR * (pseudo + OUTER_MU * fresh)
-    fresh_ref[...] = fresh
-    params_ref[...] = params
+    params, _ = step(global_rows, moment_ref[...], pseudo)
+    pseudo_ref[...] = pseudo
     weight_ref[...] = params.astype(jnp.bfloat16)
+
+
+def step(global_rows, moment_rows, pseudo):
+    fresh_moment = OUTER_MU * moment_rows + pseudo
+    fresh_params = global_rows - OUTER_LR * (pseudo + OUTER_MU * fresh_moment)
+    return (fresh_params, fresh_moment)
 
 
 def outer_update(all_local, global_params, momentum, sign_bits):
@@ -75,12 +79,86 @@
         out_shape=(
             jax.ShapeDtypeStruct((row_count, width), jnp.bfloat16),
             jax.ShapeDtypeStruct((row_count, width), jnp.float32),
-            jax.ShapeDtypeStruct((row_count, width), jnp.float32),
         ),
         in_specs=[pl.BlockSpec(memory_space=pltpu.VMEM)] * 4,
-        out_specs=[pl.BlockSpec(memory_space=pltpu.VMEM)] * 3,
+        out_specs=[pl.BlockSpec(memory_space=pltpu.VMEM)] * 2,
+        compiler_params=pltpu.CompilerParams(vmem_limit_bytes=4 * 1024 * 1024),
         cost_estimate=pl.CostEstimate(flops=20_000_000, bytes_accessed=250_000, transcendentals=0),
     )(all_local, global_params, momentum, sign_bits.reshape(1, width))
+
+
+CHUNK = 512
+PIECE_AXES = ("y0", "z0", "x0", "y1", "x1", "zh")
+
+
+def pieces_of(chunk, row_count):
+    order = ("y1", "y0", "zh", "z0", "x1", "x0")
+    sizes = [SIZES[axis] for axis in order]
+    count = CHUNK // row_count
+    for piece in range(chunk * count, (chunk + 1) * count):
+        at = dict(zip(order, np.unravel_index(piece, sizes)))
+        yield tuple(int(at[axis]) for axis in PIECE_AXES)
+
+
+def tail_kernel(core_ref, weight_ref, cot_ref, back_ref, hidden_ref, tokens_ref, inverse_ref, gain_ref, mine_ref, keys_out, grads_out, scaled_ref, keys_ref, grads_ref, sems):
+    tokens, width = tokens_ref.shape
+    row_count, half = weight_ref.shape[-2:]
+    chunks = width // CHUNK
+    cotangent = cot_ref[...]
+    keys = jnp.zeros((tokens, half), jnp.float32)
+    total = jnp.zeros((tokens, 1), jnp.float32)
+    for chunk in range(chunks):
+        columns = slice(chunk * CHUNK, (chunk + 1) * CHUNK)
+        rows = jnp.concatenate([weight_ref[at] for at in pieces_of(chunk, row_count)], axis=0)
+        back = back_ref[:, columns] + lax.dot_general(
+            cotangent, rows, (((1,), (1,)), ((), ())), preferred_element_type=jnp.float32
+        )
+        keys = keys + jnp.dot(hidden_ref[:, columns], rows, preferred_element_type=jnp.float32)
+        scaled = back * gain_ref[:, columns]
+        scaled_ref[:, columns] = scaled
+        total = total + jnp.sum(scaled * tokens_ref[:, columns].astype(jnp.float32), axis=1, keepdims=True)
+    other = keys.astype(jnp.bfloat16).astype(jnp.float32)
+    mine = mine_ref[...].astype(jnp.float32)
+    first = core_ref[0] == 0
+    keys_ref[:, :half] = jnp.where(first, mine, other).astype(jnp.bfloat16)
+    keys_ref[:, half:] = jnp.where(first, other, mine).astype(jnp.bfloat16)
+    copies = [pltpu.make_async_copy(keys_ref, keys_out, sems.at[chunks])]
+    copies[0].start()
+    inverse = inverse_ref[...]
+    centre = inverse * total / width
+    factor = inverse * inverse * centre
+    for chunk in range(chunks):
+        columns = slice(chunk * CHUNK, (chunk + 1) * CHUNK)
+        grads = inverse * scaled_ref[:, columns] - factor * tokens_ref[:, columns].astype(jnp.float32)
+        grads_ref[:, columns] = grads.astype(jnp.bfloat16)
+        copy = pltpu.make_async_copy(grads_ref.at[:, columns], grads_out.at[:, columns], sems.at[chunk])
+        copy.start()
+        copies.append(copy)
+    for copy in copies:
+        copy.wait()
+
+
+def tail(core, weight, cotangent, back, hidden, tokens, inverse, gain, keys_mine):
+    count, width = tokens.shape
+    half = keys_mine.shape[1]
+    vmem = pl.BlockSpec(memory_space=pltpu.VMEM)
+    return pl.pallas_call(
+        tail_kernel,
+        out_shape=(
+            jax.ShapeDtypeStruct((count, 2 * half), jnp.bfloat16),
+            jax.ShapeDtypeStruct((count, width), jnp.bfloat16),
+        ),
+        in_specs=[pl.BlockSpec(memory_space=pltpu.SMEM)] + [vmem] * 8,
+        out_specs=[pl.BlockSpec(memory_space=pltpu.HBM)] * 2,
+        scratch_shapes=[
+            pltpu.VMEM((count, width), jnp.float32),
+            pltpu.VMEM((count, 2 * half), jnp.bfloat16),
+            pltpu.VMEM((count, width), jnp.bfloat16),
+            pltpu.SemaphoreType.DMA((width // CHUNK + 1,)),
+        ],
+        compiler_params=pltpu.CompilerParams(vmem_limit_bytes=20 * 1024 * 1024),
+        cost_estimate=pl.CostEstimate(flops=900_000_000, bytes_accessed=12_000_000, transcendentals=0),
+    )(core.reshape(1), weight, cotangent, back, hidden, tokens, inverse, gain, keys_mine)
 
 
 def cubes():
@@ -105,7 +183,7 @@
 
 def body(tokens, gain, key_cotangent, global_params, local_params, momentum, sign_bits):
     all_local = gather(local_params[0], REPLICA, 4)
-    weight_part, new_params, new_momentum = outer_update(all_local, global_params, momentum, sign_bits)
+    weight_part, pseudo = outer_update(all_local, global_params, momentum, sign_bits)
     row_count, width = global_params.shape
 
     half = width // 2
@@ -114,30 +192,22 @@
     got = gather(mine, ("zh",), 8)
     got = gather(got, ("y1", "x1"), 4)
     got = gather(got, AXES, 8, cubes())
-    got = got.reshape(2, 2, 2, 2, 2, 8, row_count, half).transpose(3, 0, 5, 1, 4, 2, 6, 7)
-    got = got.reshape(-1, half)
+    got = got.reshape(tuple(SIZES[axis] for axis in PIECE_AXES) + (row_count, half))
     other = lax.ppermute(got, "core", [(0, 1), (1, 0)])
-
+    weight = got.transpose(3, 0, 5, 1, 4, 2, 6, 7).reshape(-1, half)
+
+    pseudo, outer, moment, _ = lax.optimization_barrier((pseudo, global_params, momentum, got))
+    new_params, new_momentum = step(outer, moment, pseudo)
     tok_float = tokens[0].astype(jnp.float32)
-    gain_vec = gain[0]
     inverse = lax.rsqrt(jnp.mean(tok_float * tok_float, axis=-1, keepdims=True) + NORM_EPS)
-    normed = tok_float * inverse
-    hidden = (normed * gain_vec).astype(jnp.bfloat16)
+    hidden = (tok_float * inverse * gain[0]).astype(jnp.bfloat16)
+    hidden = lax.optimization_barrier(hidden)
     low, high = key_cotangent[0][:, :half], key_cotangent[0][:, half:]
-
-    def both(cotangent, weight):
-        keys = jnp.dot(hidden, weight, preferred_element_type=jnp.float32)
-        back = lax.dot_general(cotangent, weight, (((1,), (1,)), ((), ())), preferred_element_type=jnp.float32)
-        return keys.astype(jnp.bfloat16), back
-
-    keys_mine, back_mine = both(jnp.where(core == 0, low, high), got)
-    keys_other, back_other = both(jnp.where(core == 0, high, low), other)
-    keys = jnp.zeros((keys_mine.shape[0], width), jnp.bfloat16)
-    keys = lax.dynamic_update_slice(keys, keys_mine, (0, core * half))
-    keys = lax.dynamic_update_slice(keys, keys_other, (0, half - core * half))
-    scaled = (back_mine + back_other) * gain_vec
-    centre = jnp.mean(scaled * normed, axis=-1, keepdims=True)
-    grads = (inverse * (scaled - normed * centre)).astype(jnp.bfloat16)
+    cot_mine = jnp.where(core == 0, low, high)
+    cot_other = jnp.where(core == 0, high, low)
+    keys_mine = jnp.dot(hidden, weight, preferred_element_type=jnp.float32).astype(jnp.bfloat16)
+    back = lax.dot_general(cot_mine, weight, (((1,), (1,)), ((), ())), preferred_element_type=jnp.float32)
+    keys, grads = tail(core, other, cot_other, back, hidden, tokens[0], inverse, gain, keys_mine)
     return (keys[None], grads[None], new_params, new_momentum)
 
 

time: 105 us -> 102 us (0.971)
  blocking collectives: 56.2 us -> 34.4 us
  waiting for transfers between devices: 7.17 us -> 26 us
  matrix products: 9.55 us -> 1.42 us
  starting transfers between devices: 20.7 us -> 26.1 us
  local copies, waits for them, and re-layouts: 4.59 us -> 7.18 us
  Pallas kernels: 1.99 us -> 3.62 us
  other arithmetic: 3.04 us -> 1.53 us
    all_to_all x3 -> x2, blocking collectives: 56.2 us -> 34.4 us  [gather(): lax.all_to_all(copies, axes, 0, 0, axis_index_groups=groups, tiled=True)]
    all_to_all x1 -> x2, waiting for transfers between devices: 7.17 us -> 26 us  [gather(): lax.all_to_all(copies, axes, 0, 0, axis_index_groups=groups, tiled=True)]
    dot_general x4 -> x2, matrix products: 9.55 us -> 1.42 us  [the longest x1 0.84 us: body(): lax.dot_general(cot_mine, weight, (((1,), (1,)), ((), ())), preferred_ele...]
    all_to_all x1 -> x2, starting transfers between devices: 17.4 us -> 21.9 us  [gather(): lax.all_to_all(copies, axes, 0, 0, axis_index_groups=groups, tiled=True)]
    pallas_call x0 -> x1, Pallas kernels: none -> 3.13 us  [tail(): pl.pallas_call(tail_kernel, out_shape=(jax.ShapeDtypeStruct((count, 2 * h...]
    broadcast_in_dim x1 -> x0, other arithmetic: 1.92 us -> none  [body(): return (keys[None], grads[None], new_params, new_momentum)]
    pallas_call x1, Pallas kernels: 1.99 us -> 0.49 us  [outer_update(): pl.pallas_call(update_kernel, out_shape=(jax.ShapeDtypeStruct((row_count,...]
    broadcast_in_dim x4, local copies, waits for them, and re-layouts: 1.6 us -> 2.92 us  [gather(): copies = jnp.broadcast_to(block[None], (count,) + block.shape)]
  transfers between devices with their start and end apart: 2 -> 3, of which waited for: 1 -> 2; matrix products, arithmetic and copies ran while one was open for 5% -> 5% of each run, Pallas kernels for 0% -> 0%
where the time goes in v5:
time: 102 us; the launch traced here: 101 us
  blocking collectives  34.4 us (34%)
  starting transfers between devices  26.1 us (26%)
  waiting for transfers between devices  26 us (25%)
  local copies, waits for them, and re-layouts  7.18 us (7%)
  Pallas kernels  3.62 us (4%)
  other arithmetic  1.53 us (2%)
  matrix products  1.42 us (1%)
    all_to_all x2, blocking collectives, gather(): lax.all_to_all(copies, axes, 0, 0, axis_index_groups=groups, tiled=True)  34.4 us
    all_to_all x2, waiting for transfers between devices, gather(): lax.all_to_all(copies, axes, 0, 0, axis_index_groups=groups, tiled=True)  26 us
    all_to_all x2, starting transfers between devices, gather(): lax.all_to_all(copies, axes, 0, 0, axis_index_groups=groups, tiled=True)  21.9 us
    ppermute x1, starting transfers between devices, body(): other = lax.ppermute(got, 'core', [(0, 1), (1, 0)])  4.23 us
    pallas_call x1, Pallas kernels, tail(): pl.pallas_call(tail_kernel, out_shape=(jax.ShapeDtypeStruct((count, 2 * h...  3.13 us
    broadcast_in_dim x4, local copies, waits for them, and re-layouts, gather(): copies = jnp.broadcast_to(block[None], (count,) + block.shape)  2.92 us
    unnamed x16, local copies, waits for them, and re-layouts  2.22 us
  transfers between devices with their start and end apart: 3, of which 2 were waited for; matrix products, arithmetic and copies ran while one was open for 5% of the time, Pallas kernels for 0%

profile of v5, /device:TPU:1, one launch (start us, length us, event | category | flops | bytes accessed | tf_op | source)
XLA Modules:
  0.0 101.0 jit_solution(7338033486446639200)
XLA Ops:
  0.6 1.4 %broadcast_in_dim.15 = bf16[4,16,512]{2,1,0:T(8,128)(2,1)} broadcast(bf16[16,512]{1,0:T(8,128)(2,1)} %bitcast.25), dimensions={1,2} | broadcast | bytes 81920 | tf_op jit(solution)/shard_map/broadcast_in_dim | solution.py:180
  2.0 17.4 %all-to-all-start = ((bf16[4,16,512]{2,1,0:T(8,128)(2,1)}), bf16[4,16,512]{2,1,0:T(8,128)(2,1)S(1)}, u32[]{:S(2)}, u32[]{:S(2)}) async-start(bf16[4,16,512]{2,1,0:T(8,128)(2,1)} %broadcast_in_dim.15), calls=%async_computation | async-start | bytes 131072 | tf_op jit(solution)/shard_map/all_to_all | solution.py:181
  19.4 7.2 %all-to-all-done.local_ref = bf16[4,16,512]{2,1,0:T(8,128)(2,1)S(1)} async-done(((bf16[4,16,512]{2,1,0:T(8,128)(2,1)}), bf16[4,16,512]{2,1,0:T(8,128)(2,1)S(1)}, u32[]{:S(2)}, u32[]{:S(2)}) %all-to-all-start) | async-done | bytes 65568 | tf_op jit(solution)/shard_map/all_to_all | solution.py:181
  26.6 0.0 copy-start.1
  26.6 0.8 copy-done.1
  27.3 0.0 copy-start.3
  27.3 0.8 copy-done.3
  28.1 0.7 copy-done.6
  28.8 0.5 shard_map.102
  29.3 21.9 %all_to_all.20 = bf16[8,16,256]{2,1,0:T(8,128)(2,1)S(1)} all-to-all(bf16[8,16,256]{2,1,0:T(8,128)(2,1)S(1)} %broadcast_in_dim.16), channel_id=1, replica_groups=mesh['yh'=2,'core'=2,'y1'=2,'y0'=2,'zh'=8,'z0'=2,'x1'=2,'x0'=2] {'zh'}, dimensions={0} | all-to-all | bytes 131072 | tf_op jit(solution)/shard_map/all_to_all | solution.py:181
  51.2 12.5 %all_to_all.21 = bf16[4,8,16,256]{3,2,1,0:T(8,128)(2,1)S(1)} all-to-all(bf16[4,8,16,256]{3,2,1,0:T(8,128)(2,1)S(1)} %broadcast_in_dim.17), channel_id=1, replica_groups=mesh['yh'=2,'core'=2,'y1'=2,'y0'=2,'zh'=8,'z0'=2,'x1'=2,'x0'=2] {'y1','x1'}, dimensions={0} | all-to-all | bytes 524288 | tf_op jit(solution)/shard_map/all_to_all | solution.py:181
  63.8 1.5 %broadcast_in_dim.36 = bf16[8,4,8,16,256]{4,3,2,1,0:T(8,128)(2,1)} broadcast(bf16[4,8,16,256]{3,2,1,0:T(8,128)(2,1)S(1)} %all_to_all.21), dimensions={1,2,3,4} | broadcast | bytes 2359296 | tf_op jit(solution)/shard_map/broadcast_in_dim | solution.py:180
  65.3 4.5 %all-to-all-start.3 = ((bf16[8,4,8,16,256]{4,3,2,1,0:T(8,128)(2,1)}), bf16[8,4,8,16,256]{4,3,2,1,0:T(8,128)(2,1)}, u32[]{:S(2)}, u32[]{:S(2)}) async-start(bf16[8,4,8,16,256]{4,3,2,1,0:T(8,128)(2,1)} %broadcast_in_dim.36), calls=%async_computation.3 | async-start | bytes 4194304 | tf_op jit(solution)/shard_map/all_to_all | solution.py:181
  69.8 0.0 copy-done
  69.8 0.0 copy-start.7
  69.8 0.4 fusion
  70.2 0.1 copy.12.inverse_ref
  70.3 18.8 %all-to-all-done.3 = bf16[8,4,8,16,256]{4,3,2,1,0:T(8,128)(2,1)} async-done(((bf16[8,4,8,16,256]{4,3,2,1,0:T(8,128)(2,1)}), bf16[8,4,8,16,256]{4,3,2,1,0:T(8,128)(2,1)}, u32[]{:S(2)}, u32[]{:S(2)}) %all-to-all-start.3) | async-done | bytes 2097184 | tf_op jit(solution)/shard_map/all_to_all | solution.py:181
  89.1 4.2 %collective-permute-start = (bf16[2,2,2,2,2,8,16,256]{7,6,5,4,3,2,1,0:T(8,128)(2,1)}, bf16[2,2,2,2,2,8,16,256]{7,6,5,4,3,2,1,0:T(8,128)(2,1)S(1)}, u32[]{:S(2)}, u32[]{:S(2)}) collective-permute-start(bf16[2,2,2,2,2,8,16,256]{7,6,5,4,3,2,1,0:T(8,128)(2,1)} %bitcast.3), channel_id=1, source_target_pairs={{0,256},{256,0},{1,257},{257,1},{2,258},{258,2},{3,259},{259,3},{4... | collective-permute-start | bytes 6291464 | tf_op jit(solution)/shard_map/ppermute | solution.py:196
  93.4 0.0 copy-done.5
  93.4 0.5 fusion.2.hidden_ref
  93.9 0.0 copy-done.7
  93.9 0.0 copy-start.2
  93.9 0.0 copy-start.4
  93.9 1.9 %copy.11 = bf16[2,2,8,2,2,2,16,256]{7,6,5,4,3,2,1,0:T(8,128)(2,1)S(1)} copy(bf16[2,2,8,2,2,2,16,256]{7,6,2,4,0,5,3,1:T(8,128)(2,1)} %bitcast.5) | data formatting | bytes 4194304 | tf_op jit(solution)/shard_map/transpose | solution.py:197
  95.8 0.0 copy-done.2
  95.8 0.0 copy-done.4
  95.8 0.6 multiply_subtract_fusion
  96.5 0.6 convolution_convert_fusion.mine_ref
  97.1 0.8 fusion.3.back_ref
  97.9 0.0 collective-permute-done.weight_ref
  97.9 3.1 %shard_map.103 = (bf16[192,512]{1,0:T(8,128)(2,1)}, bf16[192,4096]{1,0:T(8,128)(2,1)}) custom-call(s32[1]{0:T(128)} %bitcast.core_ref, bf16[2,2,2,2,2,8,16,256]{7,6,5,4,3,2,1,0:T(8,128)(2,1)S(1)} %collective-permute-done.weight_ref, bf16[192,256]{1,0:T(8,128)(2,1)S(1)} %broadcast_select_fusion.cot_ref, f32[192,4096]{1,0:T(8,128)S(1)} %fusion.3.back_ref, ...), custom_call_target="tpu_custom_call" | custom-call | flops 900000000 | bytes 12000000 | tf_op jit(solution)/shard_map/pallas_call | solution.py:145
  (8 shorter events, 0.1 us)
Async XLA Ops:
  2.0 24.6 %all-to-all-start = ((bf16[4,16,512]{2,1,0:T(8,128)(2,1)}), bf16[4,16,512]{2,1,0:T(8,128)(2,1)S(1)}, u32[]{:S(2)}, u32[]{:S(2)}) async-start(bf16[4,16,512]{2,1,0:T(8,128)(2,1)} %broadcast_in_dim.15), calls=%async_computation | async-start | bytes 131072 | tf_op jit(solution)/shard_map/all_to_all | solution.py:181
  26.6 0.8 copy-start.1
  27.3 0.8 copy-start.3
  28.1 0.7 copy-start.6
  65.3 4.5 %copy-start = (bf16[1,192,4096]{2,1,0:T(8,128)(2,1)S(1)}, bf16[1,192,4096]{2,1,0:T(8,128)(2,1)}, u32[]{:S(2)}) copy-start(bf16[1,192,4096]{2,1,0:T(8,128)(2,1)} %param.7) | copy-start | bytes 4718596
  65.3 28.1 %copy-start.5 = (f32[1,4096]{1,0:T(1,128)S(1)}, f32[1,4096]{1,0:T(1,128)}, u32[]{:S(2)}) copy-start(f32[1,4096]{1,0:T(1,128)} %gain_ref.1) | copy-start | bytes 49156
  65.3 23.8 %all-to-all-start.3 = ((bf16[8,4,8,16,256]{4,3,2,1,0:T(8,128)(2,1)}), bf16[8,4,8,16,256]{4,3,2,1,0:T(8,128)(2,1)}, u32[]{:S(2)}, u32[]{:S(2)}) async-start(bf16[8,4,8,16,256]{4,3,2,1,0:T(8,128)(2,1)} %broadcast_in_dim.36), calls=%async_computation.3 | async-start | bytes 4194304 | tf_op jit(solution)/shard_map/all_to_all | solution.py:181
  69.8 24.1 %copy-start.7 = (bf16[1,192,512]{2,1,0:T(8,128)(2,1)S(1)}, bf16[1,192,512]{2,1,0:T(8,128)(2,1)}, u32[]{:S(2)}) copy-start(bf16[1,192,512]{2,1,0:T(8,128)(2,1)} %param.9) | copy-start | bytes 589828
  89.1 8.8 %collective-permute-start = (bf16[2,2,2,2,2,8,16,256]{7,6,5,4,3,2,1,0:T(8,128)(2,1)}, bf16[2,2,2,2,2,8,16,256]{7,6,5,4,3,2,1,0:T(8,128)(2,1)S(1)}, u32[]{:S(2)}, u32[]{:S(2)}) collective-permute-start(bf16[2,2,2,2,2,8,16,256]{7,6,5,4,3,2,1,0:T(8,128)(2,1)} %bitcast.3), channel_id=1, source_target_pairs={{0,256},{256,0},{1,257},{257,1},{2,258},{258,2},{3,259},{259,3},{4... | collective-permute-start | bytes 6291464 | tf_op jit(solution)/shard_map/ppermute | solution.py:196
  93.9 1.9 %copy-start.2 = (f32[16,512]{1,0:T(8,128)S(1)}, f32[16,512]{1,0:T(8,128)}, u32[]{:S(2)}) copy-start(f32[16,512]{1,0:T(8,128)} %global_ref.1) | copy-start | bytes 98308
  93.9 1.9 %copy-start.4 = (f32[16,512]{1,0:T(8,128)S(1)}, f32[16,512]{1,0:T(8,128)}, u32[]{:S(2)}) copy-start(f32[16,512]{1,0:T(8,128)} %moment_ref.1) | copy-start | bytes 98308

commit v6 on v5

--- a/solution.py
+++ b/solution.py
@@ -40,12 +40,12 @@
     return total * (1.0 / math.sqrt(HB))
 
 
-def update_kernel(local_ref, global_ref, moment_ref, bits_ref, weight_ref, pseudo_ref):
+def update_kernel(local_ref, held_ref, weight_ref, pseudo_ref):
     replicas, row_count, width = local_ref.shape
     count = width // HB
     matrix = signs()
-    sign_vec = (2 * bits_ref[...] - 1).astype(jnp.float32)
-    global_rows = global_ref[...]
+    sign_vec = held_ref[2]
+    global_rows = held_ref[0]
     pieces = []
     for replica in range(replicas):
         drift = (global_rows - local_ref[replica].astype(jnp.float32)) * sign_vec
@@ -61,7 +61,7 @@
     restored = rotate(summed / replicas, matrix)
     restored = jnp.concatenate([restored[at * row_count : (at + 1) * row_count] for at in range(count)], axis=1)
     pseudo = restored * sign_vec
-    params, _ = step(global_rows, moment_ref[...], pseudo)
+    params, _ = step(global_rows, held_ref[1], pseudo)
     pseudo_ref[...] = pseudo
     weight_ref[...] = params.astype(jnp.bfloat16)
 
@@ -72,19 +72,19 @@
     return (fresh_params, fresh_moment)
 
 
-def outer_update(all_local, global_params, momentum, sign_bits):
-    row_count, width = global_params.shape
+def outer_update(all_local, held):
+    row_count, width = held.shape[1:]
     return pl.pallas_call(
         update_kernel,
         out_shape=(
             jax.ShapeDtypeStruct((row_count, width), jnp.bfloat16),
             jax.ShapeDtypeStruct((row_count, width), jnp.float32),
         ),
-        in_specs=[pl.BlockSpec(memory_space=pltpu.VMEM)] * 4,
+        in_specs=[pl.BlockSpec(memory_space=pltpu.VMEM)] * 2,
         out_specs=[pl.BlockSpec(memory_space=pltpu.VMEM)] * 2,
         compiler_params=pltpu.CompilerParams(vmem_limit_bytes=4 * 1024 * 1024),
         cost_estimate=pl.CostEstimate(flops=20_000_000, bytes_accessed=250_000, transcendentals=0),
-    )(all_local, global_params, momentum, sign_bits.reshape(1, width))
+    )(all_local, held)
 
 
 CHUNK = 512
@@ -100,15 +100,66 @@
         yield tuple(int(at[axis]) for axis in PIECE_AXES)
 
 
+def columns_of(core, half):
+    return pl.ds(pl.multiple_of(core * half, half), half)
+
+
+def own_kernel(core_ref, weight_ref, cot_ref, tokens_ref, gain_ref, held_ref, pseudo_ref, back_ref, hidden_ref, inverse_ref, keys_ref, params_ref, fresh_ref):
+    tokens, width = tokens_ref.shape
+    row_count, half = weight_ref.shape[-2:]
+    parts = [slice(at, at + CHUNK) for at in range(0, width, CHUNK)]
+    total = jnp.zeros((tokens, 1), jnp.float32)
+    for columns in parts:
+        values = tokens_ref[:, columns].astype(jnp.float32)
+        total = total + jnp.sum(values * values, axis=1, keepdims=True)
+    inverse = lax.rsqrt(total / width + NORM_EPS)
+    inverse_ref[...] = inverse
+    cotangent = cot_ref[:, columns_of(core_ref[0], half)]
+    keys = jnp.zeros((tokens, half), jnp.float32)
+    for chunk, columns in enumerate(parts):
+        rows = jnp.concatenate([weight_ref[at] for at in pieces_of(chunk, row_count)], axis=0)
+        back_ref[:, columns] = lax.dot_general(
+            cotangent, rows, (((1,), (1,)), ((), ())), preferred_element_type=jnp.float32
+        )
+        hidden = (tokens_ref[:, columns].astype(jnp.float32) * inverse * gain_ref[:, columns]).astype(jnp.bfloat16)
+        hidden_ref[:, columns] = hidden
+        keys = keys + jnp.dot(hidden, rows, preferred_element_type=jnp.float32)
+    keys_ref[...] = keys.astype(jnp.bfloat16)
+    params, fresh = step(held_ref[0], held_ref[1], pseudo_ref[...])
+    params_ref[...] = params
+    fresh_ref[...] = fresh
+
+
+def own_half(core, weight, cotangent, tokens, gain, held, pseudo):
+    count, width = tokens.shape
+    half = weight.shape[-1]
+    vmem = pl.BlockSpec(memory_space=pltpu.VMEM)
+    return pl.pallas_call(
+        own_kernel,
+        out_shape=(
+            jax.ShapeDtypeStruct((count, width), jnp.float32),
+            jax.ShapeDtypeStruct((count, width), jnp.bfloat16),
+            jax.ShapeDtypeStruct((count, 1), jnp.float32),
+            jax.ShapeDtypeStruct((count, half), jnp.bfloat16),
+            jax.ShapeDtypeStruct(pseudo.shape, jnp.float32),
+            jax.ShapeDtypeStruct(pseudo.shape, jnp.float32),
+        ),
+        in_specs=[pl.BlockSpec(memory_space=pltpu.SMEM)] + [vmem] * 6,
+        out_specs=[vmem] * 6,
+        compiler_params=pltpu.CompilerParams(vmem_limit_bytes=24 * 1024 * 1024),
+        cost_estimate=pl.CostEstimate(flops=900_000_000, bytes_accessed=12_000_000, transcendentals=0),
+    )(core.reshape(1), weight, cotangent, tokens, gain, held, pseudo)
+
+
 def tail_kernel(core_ref, weight_ref, cot_ref, back_ref, hidden_ref, tokens_ref, inverse_ref, gain_ref, mine_ref, keys_out, grads_out, scaled_ref, keys_ref, grads_ref, sems):
     tokens, width = tokens_ref.shape
     row_count, half = weight_ref.shape[-2:]
-    chunks = width // CHUNK
-    cotangent = cot_ref[...]
+    parts = [slice(at, at + CHUNK) for at in range(0, width, CHUNK)]
+    core = core_ref[0]
+    cotangent = cot_ref[:, columns_of(1 - core, half)]
     keys = jnp.zeros((tokens, half), jnp.float32)
     total = jnp.zeros((tokens, 1), jnp.float32)
-    for chunk in range(chunks):
-        columns = slice(chunk * CHUNK, (chunk + 1) * CHUNK)
+    for chunk, columns in enumerate(parts):
         rows = jnp.concatenate([weight_ref[at] for at in pieces_of(chunk, row_count)], axis=0)
         back = back_ref[:, columns] + lax.dot_general(
             cotangent, rows, (((1,), (1,)), ((), ())), preferred_element_type=jnp.float32
@@ -117,18 +168,14 @@
         scaled = back * gain_ref[:, columns]
         scaled_ref[:, columns] = scaled
         total = total + jnp.sum(scaled * tokens_ref[:, columns].astype(jnp.float32), axis=1, keepdims=True)
-    other = keys.astype(jnp.bfloat16).astype(jnp.float32)
-    mine = mine_ref[...].astype(jnp.float32)
-    first = core_ref[0] == 0
-    keys_ref[:, :half] = jnp.where(first, mine, other).astype(jnp.bfloat16)
-    keys_ref[:, half:] = jnp.where(first, other, mine).astype(jnp.bfloat16)
-    copies = [pltpu.make_async_copy(keys_ref, keys_out, sems.at[chunks])]
+    keys_ref[:, columns_of(core, half)] = mine_ref[...]
+    keys_ref[:, columns_of(1 - core, half)] = keys.astype(jnp.bfloat16)
+    copies = [pltpu.make_async_copy(keys_ref, keys_out, sems.at[len(parts)])]
     copies[0].start()
     inverse = inverse_ref[...]
     centre = inverse * total / width
     factor = inverse * inverse * centre
-    for chunk in range(chunks):
-        columns = slice(chunk * CHUNK, (chunk + 1) * CHUNK)
+    for chunk, columns in enumerate(parts):
         grads = inverse * scaled_ref[:, columns] - factor * tokens_ref[:, columns].astype(jnp.float32)
         grads_ref[:, columns] = grads.astype(jnp.bfloat16)
         copy = pltpu.make_async_copy(grads_ref.at[:, columns], grads_out.at[:, columns], sems.at[chunk])
@@ -183,8 +230,10 @@
 
 def body(tokens, gain, key_cotangent, global_params, local_params, momentum, sign_bits):
     all_local = gather(local_params[0], REPLICA, 4)
-    weight_part, pseudo = outer_update(all_local, global_params, momentum, sign_bits)
     row_count, width = global_params.shape
+    sign_vec = jnp.broadcast_to((2 * sign_bits - 1).astype(jnp.float32), (row_count, width))
+    held = lax.optimization_barrier(jnp.stack([global_params, momentum, sign_vec]))
+    weight_part, pseudo = outer_update(all_local, held)
 
     half = width // 2
     core = lax.axis_index("core")
@@ -194,20 +243,11 @@
     got = gather(got, AXES, 8, cubes())
     got = got.reshape(tuple(SIZES[axis] for axis in PIECE_AXES) + (row_count, half))
     other = lax.ppermute(got, "core", [(0, 1), (1, 0)])
-    weight = got.transpose(3, 0, 5, 1, 4, 2, 6, 7).reshape(-1, half)
-
-    pseudo, outer, moment, _ = lax.optimization_barrier((pseudo, global_params, momentum, got))
-    new_params, new_momentum = step(outer, moment, pseudo)
-    tok_float = tokens[0].astype(jnp.float32)
-    inverse = lax.rsqrt(jnp.mean(tok_float * tok_float, axis=-1, keepdims=True) + NORM_EPS)
-    hidden = (tok_float * inverse * gain[0]).astype(jnp.bfloat16)
-    hidden = lax.optimization_barrier(hidden)
-    low, high = key_cotangent[0][:, :half], key_cotangent[0][:, half:]
-    cot_mine = jnp.where(core == 0, low, high)
-    cot_other = jnp.where(core == 0, high, low)
-    keys_mine = jnp.dot(hidden, weight, preferred_element_type=jnp.float32).astype(jnp.bfloat16)
-    back = lax.dot_general(cot_mine, weight, (((1,), (1,)), ((), ())), preferred_element_type=jnp.float32)
-    keys, grads = tail(core, other, cot_other, back, hidden, tokens[0], inverse, gain, keys_mine)
+
+    rows, cotangent = tokens[0], key_cotangent[0]
+    own = own_half(core, got, cotangent, rows, gain, held, pseudo)
+    back, hidden, inverse, keys_mine, new_params, new_momentum = own
+    keys, grads = tail(core, other, cotangent, back, hidden, rows, inverse, gain, keys_mine)
     return (keys[None], grads[None], new_params, new_momentum)
 
 

time: 102 us -> 94.3 us (0.925)
  blocking collectives: 34.4 us -> 56.3 us
  waiting for transfers between devices: 26 us -> 7.36 us
  local copies, waits for them, and re-layouts: 7.18 us -> 1.63 us
  starting transfers between devices: 26.1 us -> 20.7 us
  Pallas kernels: 3.62 us -> 5.61 us
  matrix products: 1.42 us -> 0 us
    all_to_all x2 -> x3, blocking collectives: 34.4 us -> 56.3 us  [gather(): lax.all_to_all(copies, axes, 0, 0, axis_index_groups=groups, tiled=True)]
    all_to_all x2 -> x1, waiting for transfers between devices: 26 us -> 5.69 us  [gather(): lax.all_to_all(copies, axes, 0, 0, axis_index_groups=groups, tiled=True)]
    all_to_all x2 -> x1, starting transfers between devices: 21.9 us -> 17.4 us  [gather(): lax.all_to_all(copies, axes, 0, 0, axis_index_groups=groups, tiled=True)]
    unnamed x16 -> x6, local copies, waits for them, and re-layouts: 2.22 us -> 0.02 us
    pallas_call x0 -> x1, Pallas kernels: none -> 2.07 us  [own_half(): pl.pallas_call(own_kernel, out_shape=(jax.ShapeDtypeStruct((count, width)...]
    transpose x1 -> x0, local copies, waits for them, and re-layouts: 1.91 us -> none  [body(): weight = got.transpose(3, 0, 5, 1, 4, 2, 6, 7).reshape(-1, half)]
    ppermute x1, waiting for transfers between devices: 0.01 us -> 1.66 us  [body(): other = lax.ppermute(got, 'core', [(0, 1), (1, 0)])]
    dot_general x2 -> x0, matrix products: 1.42 us -> none  [the longest x1 0.84 us: body(): lax.dot_general(cot_mine, weight, (((1,), (1,)), ((), ())), preferred_ele...]
  transfers between devices with their start and end apart: 3 -> 2, of which waited for: 2 -> 2; matrix products, arithmetic and copies ran while one was open for 5% -> 2% of each run, Pallas kernels for 0% -> 2%
where the time goes in v6:
time: 94.3 us; the launch traced here: 93.8 us
  blocking collectives  56.3 us (60%)
  starting transfers between devices  20.7 us (22%)
  waiting for transfers between devices  7.36 us (8%)
  Pallas kernels  5.61 us (6%)
  local copies, waits for them, and re-layouts  1.63 us (2%)
  other arithmetic  1.47 us (2%)
    all_to_all x3, blocking collectives, gather(): lax.all_to_all(copies, axes, 0, 0, axis_index_groups=groups, tiled=True)  56.3 us
    all_to_all x1, starting transfers between devices, gather(): lax.all_to_all(copies, axes, 0, 0, axis_index_groups=groups, tiled=True)  17.4 us
    all_to_all x1, waiting for transfers between devices, gather(): lax.all_to_all(copies, axes, 0, 0, axis_index_groups=groups, tiled=True)  5.69 us
    ppermute x1, starting transfers between devices, body(): other = lax.ppermute(got, 'core', [(0, 1), (1, 0)])  3.31 us
    pallas_call x1, Pallas kernels, tail(): pl.pallas_call(tail_kernel, out_shape=(jax.ShapeDtypeStruct((count, 2 * h...  3.04 us
    pallas_call x1, Pallas kernels, own_half(): pl.pallas_call(own_kernel, out_shape=(jax.ShapeDtypeStruct((count, width)...  2.07 us
  transfers between devices with their start and end apart: 2, of which 2 were waited for; matrix products, arithmetic and copies ran while one was open for 2% of the time, Pallas kernels for 2%

profile of v6, /device:TPU:1, one launch (start us, length us, event | category | flops | bytes accessed | tf_op | source)
XLA Modules:
  0.0 93.8 jit_solution(3757916074117863727)
XLA Ops:
  0.6 1.4 %broadcast_in_dim.15 = bf16[4,16,512]{2,1,0:T(8,128)(2,1)} broadcast(bf16[16,512]{1,0:T(8,128)(2,1)} %bitcast.17), dimensions={1,2} | broadcast | bytes 81920 | tf_op jit(solution)/shard_map/broadcast_in_dim | solution.py:227
  2.0 17.4 %all-to-all-start = ((bf16[4,16,512]{2,1,0:T(8,128)(2,1)}), bf16[4,16,512]{2,1,0:T(8,128)(2,1)S(1)}, u32[]{:S(2)}, u32[]{:S(2)}) async-start(bf16[4,16,512]{2,1,0:T(8,128)(2,1)} %broadcast_in_dim.15), calls=%async_computation | async-start | bytes 131072 | tf_op jit(solution)/shard_map/all_to_all | solution.py:228
  19.4 0.7 add_convert_fusion
  20.1 0.8 pad_maximum_fusion.held_ref
  20.9 5.7 %all-to-all-done.local_ref = bf16[4,16,512]{2,1,0:T(8,128)(2,1)S(1)} async-done(((bf16[4,16,512]{2,1,0:T(8,128)(2,1)}), bf16[4,16,512]{2,1,0:T(8,128)(2,1)S(1)}, u32[]{:S(2)}, u32[]{:S(2)}) %all-to-all-start) | async-done | bytes 65568 | tf_op jit(solution)/shard_map/all_to_all | solution.py:228
  26.6 0.5 shard_map.102
  27.1 21.9 %all_to_all.20 = bf16[8,16,256]{2,1,0:T(8,128)(2,1)S(1)} all-to-all(bf16[8,16,256]{2,1,0:T(8,128)(2,1)S(1)} %broadcast_in_dim.16), channel_id=1, replica_groups=mesh['yh'=2,'core'=2,'y1'=2,'y0'=2,'zh'=8,'z0'=2,'x1'=2,'x0'=2] {'zh'}, dimensions={0} | all-to-all | bytes 131072 | tf_op jit(solution)/shard_map/all_to_all | solution.py:228
  49.0 12.5 %all_to_all.21 = bf16[4,8,16,256]{3,2,1,0:T(8,128)(2,1)S(1)} all-to-all(bf16[4,8,16,256]{3,2,1,0:T(8,128)(2,1)S(1)} %broadcast_in_dim.34), channel_id=1, replica_groups=mesh['yh'=2,'core'=2,'y1'=2,'y0'=2,'zh'=8,'z0'=2,'x1'=2,'x0'=2] {'y1','x1'}, dimensions={0} | all-to-all | bytes 524288 | tf_op jit(solution)/shard_map/all_to_all | solution.py:228
  61.6 0.2 broadcast_in_dim.35
  61.8 0.0 copy-start
  61.8 0.0 copy-start.1
  61.8 0.0 copy-start.2
  61.8 21.9 %all_to_all.22 = bf16[8,4,8,16,256]{4,3,2,1,0:T(8,128)(2,1)S(1)} all-to-all(bf16[8,4,8,16,256]{4,3,2,1,0:T(8,128)(2,1)S(1)} %broadcast_in_dim.35), channel_id=1, replica_groups={{0,1,4,5,64,65,68,69},{2,3,6,7,66,67,70,71},{8,9,12,13,72,73,76,77},{10..., dimensions={0} | all-to-all | bytes 4194304 | tf_op jit(solution)/shard_map/all_to_all | solution.py:228
  83.7 3.3 %collective-permute-start = (bf16[2,2,2,2,2,8,16,256]{7,6,5,4,3,2,1,0:T(8,128)(2,1)S(1)}, bf16[2,2,2,2,2,8,16,256]{7,6,5,4,3,2,1,0:T(8,128)(2,1)S(1)}, u32[]{:S(2)}, u32[]{:S(2)}) collective-permute-start(bf16[2,2,2,2,2,8,16,256]{7,6,5,4,3,2,1,0:T(8,128)(2,1)S(1)} %bitcast.9), channel_id=1, source_target_pairs={{0,256},{256,0},{1,257},{257,1},{2,258},{258,2},{3,259},{259,3},{4... | collective-permute-start | bytes 6291464 | tf_op jit(solution)/shard_map/ppermute | solution.py:245
  87.0 0.0 copy-done
  87.0 0.0 copy-done.1
  87.0 0.0 copy-done.2
  87.0 2.1 %shard_map.103 = (f32[192,4096]{1,0:T(8,128)S(1)}, bf16[192,4096]{1,0:T(8,128)(2,1)S(1)}, f32[192,1]{1,0:T(8,128)S(1)}, bf16[192,256]{1,0:T(8,128)(2,1)S(1)}, f32[16,512]{1,0:T(8,128)}, /*index=5*/f32[16,512]{1,0:T(8,128)}) custom-call(s32[1]{0:T(128)} %bitcast.core_ref, bf16[2,2,2,2,2,8,16,256]{7,6,5,4,3,2,1,0:T(8,128)(2,1)S(1)} %bitcast.10, ...), custom_call_target="tpu_custom_call" | custom-call | flops 900000000 | bytes 12000000 | tf_op jit(solution)/shard_map/pallas_call | solution.py:137
  89.1 1.7 %collective-permute-done.weight_ref = bf16[2,2,2,2,2,8,16,256]{7,6,5,4,3,2,1,0:T(8,128)(2,1)S(1)} collective-permute-done((bf16[2,2,2,2,2,8,16,256]{7,6,5,4,3,2,1,0:T(8,128)(2,1)S(1)}, bf16[2,2,2,2,2,8,16,256]{7,6,5,4,3,2,1,0:T(8,128)(2,1)S(1)}, u32[]{:S(2)}, u32[]{:S(2)}) %collective-permute-start) | collective-permute-done | bytes 2097184 | tf_op jit(solution)/shard_map/ppermute | solution.py:245
  90.8 3.0 %shard_map.104 = (bf16[192,512]{1,0:T(8,128)(2,1)}, bf16[192,4096]{1,0:T(8,128)(2,1)}) custom-call(s32[1]{0:T(128)} %bitcast.core_ref, bf16[2,2,2,2,2,8,16,256]{7,6,5,4,3,2,1,0:T(8,128)(2,1)S(1)} %collective-permute-done.weight_ref, bf16[192,512]{1,0:T(8,128)(2,1)S(1)} %bitcast.14, f32[192,4096]{1,0:T(8,128)S(1)} %get-tuple-element.16.back_ref, ...), custom_call_target="tpu_custom_call" | custom-call | flops 900000000 | bytes 12000000 | tf_op jit(solution)/shard_map/pallas_call | solution.py:192
  (4 shorter events, 0.0 us)
Async XLA Ops:
  2.0 24.6 %all-to-all-start = ((bf16[4,16,512]{2,1,0:T(8,128)(2,1)}), bf16[4,16,512]{2,1,0:T(8,128)(2,1)S(1)}, u32[]{:S(2)}, u32[]{:S(2)}) async-start(bf16[4,16,512]{2,1,0:T(8,128)(2,1)} %broadcast_in_dim.15), calls=%async_computation | async-start | bytes 131072 | tf_op jit(solution)/shard_map/all_to_all | solution.py:228
  61.8 25.2 %copy-start = (bf16[1,192,4096]{2,1,0:T(8,128)(2,1)S(1)}, bf16[1,192,4096]{2,1,0:T(8,128)(2,1)}, u32[]{:S(2)}) copy-start(bf16[1,192,4096]{2,1,0:T(8,128)(2,1)} %param.7) | copy-start | bytes 4718596
  61.8 25.2 %copy-start.1 = (bf16[1,192,512]{2,1,0:T(8,128)(2,1)S(1)}, bf16[1,192,512]{2,1,0:T(8,128)(2,1)}, u32[]{:S(2)}) copy-start(bf16[1,192,512]{2,1,0:T(8,128)(2,1)} %param.9) | copy-start | bytes 589828
  61.8 25.2 %copy-start.2 = (f32[1,4096]{1,0:T(1,128)S(1)}, f32[1,4096]{1,0:T(1,128)}, u32[]{:S(2)}) copy-start(f32[1,4096]{1,0:T(1,128)} %gain_ref.3) | copy-start | bytes 49156
  83.7 7.1 %collective-permute-start = (bf16[2,2,2,2,2,8,16,256]{7,6,5,4,3,2,1,0:T(8,128)(2,1)S(1)}, bf16[2,2,2,2,2,8,16,256]{7,6,5,4,3,2,1,0:T(8,128)(2,1)S(1)}, u32[]{:S(2)}, u32[]{:S(2)}) collective-permute-start(bf16[2,2,2,2,2,8,16,256]{7,6,5,4,3,2,1,0:T(8,128)(2,1)S(1)} %bitcast.9), channel_id=1, source_target_pairs={{0,256},{256,0},{1,257},{257,1},{2,258},{258,2},{3,259},{259,3},{4... | collective-permute-start | bytes 6291464 | tf_op jit(solution)/shard_map/ppermute | solution.py:245

commit v7 on v6

--- a/solution.py
+++ b/solution.py
@@ -158,7 +158,7 @@
     core = core_ref[0]
     cotangent = cot_ref[:, columns_of(1 - core, half)]
     keys = jnp.zeros((tokens, half), jnp.float32)
-    total = jnp.zeros((tokens, 1), jnp.float32)
+    total = jnp.zeros((tokens, HB), jnp.float32)
     for chunk, columns in enumerate(parts):
         rows = jnp.concatenate([weight_ref[at] for at in pieces_of(chunk, row_count)], axis=0)
         back = back_ref[:, columns] + lax.dot_general(
@@ -167,13 +167,15 @@
         keys = keys + jnp.dot(hidden_ref[:, columns], rows, preferred_element_type=jnp.float32)
         scaled = back * gain_ref[:, columns]
         scaled_ref[:, columns] = scaled
-        total = total + jnp.sum(scaled * tokens_ref[:, columns].astype(jnp.float32), axis=1, keepdims=True)
+        product = scaled * tokens_ref[:, columns].astype(jnp.float32)
+        for at in range(0, CHUNK, HB):
+            total = total + product[:, at : at + HB]
     keys_ref[:, columns_of(core, half)] = mine_ref[...]
     keys_ref[:, columns_of(1 - core, half)] = keys.astype(jnp.bfloat16)
     copies = [pltpu.make_async_copy(keys_ref, keys_out, sems.at[len(parts)])]
     copies[0].start()
     inverse = inverse_ref[...]
-    centre = inverse * total / width
+    centre = inverse * jnp.sum(total, axis=1, keepdims=True) / width
     factor = inverse * inverse * centre
     for chunk, columns in enumerate(parts):
         grads = inverse * scaled_ref[:, columns] - factor * tokens_ref[:, columns].astype(jnp.float32)
@@ -208,6 +210,21 @@
     )(core.reshape(1), weight, cotangent, back, hidden, tokens, inverse, gain, keys_mine)
 
 
+def place(core, y, z, x):
+    return (((y // 4 * 2 + core) * 4 + y % 4) * 16 + z) * 4 + x
+
+
+def squares():
+    groups = []
+    for core in range(2):
+        for y in (0, 1, 4, 5):
+            pair = (y, (y + 2 - 4 * core) % 8)
+            for z in range(16):
+                for x in range(2):
+                    groups.append([place(core, y_at, z, x_at) for y_at in pair for x_at in (x, x + 2)])
+    return groups
+
+
 def cubes():
     groups = []
     for core in range(2):
@@ -217,8 +234,7 @@
                     group = []
                     for odd in np.ndindex(2, 2, 2):
                         step = [bit * (1 - 2 * core) for bit in odd]
-                        y_at, z_at, x_at = (y + step[0]) % 8, (z + step[1]) % 16, (x + step[2]) % 4
-                        group.append((((y_at // 4 * 2 + core) * 4 + y_at % 4) * 16 + z_at) * 4 + x_at)
+                        group.append(place(core, (y + step[0]) % 8, (z + step[1]) % 16, (x + step[2]) % 4))
                     groups.append(group)
     return groups
 
@@ -239,7 +255,7 @@
     core = lax.axis_index("core")
     mine = jnp.where(core == 0, weight_part[:, :half], weight_part[:, half:])
     got = gather(mine, ("zh",), 8)
-    got = gather(got, ("y1", "x1"), 4)
+    got = gather(got, AXES, 4, squares())
     got = gather(got, AXES, 8, cubes())
     got = got.reshape(tuple(SIZES[axis] for axis in PIECE_AXES) + (row_count, half))
     other = lax.ppermute(got, "core", [(0, 1), (1, 0)])

time: 94.3 us -> 94.3 us (level)
  no operation moved by 1% of the time
where the time goes in v7:
time: 94.3 us; the launch traced here: 93.8 us
  blocking collectives  56.1 us (59%)
  starting transfers between devices  20.9 us (22%)
  waiting for transfers between devices  7.36 us (8%)
  Pallas kernels  5.59 us (6%)
  local copies, waits for them, and re-layouts  1.63 us (2%)
  other arithmetic  1.47 us (2%)
    all_to_all x3, blocking collectives, gather(): lax.all_to_all(copies, axes, 0, 0, axis_index_groups=groups, tiled=True)  56.1 us
    all_to_all x1, starting transfers between devices, gather(): lax.all_to_all(copies, axes, 0, 0, axis_index_groups=groups, tiled=True)  17.4 us
    all_to_all x1, waiting for transfers between devices, gather(): lax.all_to_all(copies, axes, 0, 0, axis_index_groups=groups, tiled=True)  5.69 us
    ppermute x1, starting transfers between devices, body(): other = lax.ppermute(got, 'core', [(0, 1), (1, 0)])  3.5 us
    pallas_call x1, Pallas kernels, tail(): pl.pallas_call(tail_kernel, out_shape=(jax.ShapeDtypeStruct((count, 2 * h...  3.02 us
    pallas_call x1, Pallas kernels, own_half(): pl.pallas_call(own_kernel, out_shape=(jax.ShapeDtypeStruct((count, width)...  2.07 us
  transfers between devices with their start and end apart: 2, of which 2 were waited for; matrix products, arithmetic and copies ran while one was open for 2% of the time, Pallas kernels for 2%

profile of v7, /device:TPU:1, one launch (start us, length us, event | category | flops | bytes accessed | tf_op | source)
XLA Modules:
  0.0 93.8 jit_solution(3984306243033143870)
XLA Ops:
  0.6 1.4 %broadcast_in_dim.15 = bf16[4,16,512]{2,1,0:T(8,128)(2,1)} broadcast(bf16[16,512]{1,0:T(8,128)(2,1)} %bitcast.17), dimensions={1,2} | broadcast | bytes 81920 | tf_op jit(solution)/shard_map/broadcast_in_dim | solution.py:243
  2.0 17.4 %all-to-all-start = ((bf16[4,16,512]{2,1,0:T(8,128)(2,1)}), bf16[4,16,512]{2,1,0:T(8,128)(2,1)S(1)}, u32[]{:S(2)}, u32[]{:S(2)}) async-start(bf16[4,16,512]{2,1,0:T(8,128)(2,1)} %broadcast_in_dim.15), calls=%async_computation | async-start | bytes 131072 | tf_op jit(solution)/shard_map/all_to_all | solution.py:244
  19.4 0.7 add_convert_fusion
  20.1 0.8 pad_maximum_fusion.held_ref
  20.9 5.7 %all-to-all-done.local_ref = bf16[4,16,512]{2,1,0:T(8,128)(2,1)S(1)} async-done(((bf16[4,16,512]{2,1,0:T(8,128)(2,1)}), bf16[4,16,512]{2,1,0:T(8,128)(2,1)S(1)}, u32[]{:S(2)}, u32[]{:S(2)}) %all-to-all-start) | async-done | bytes 65568 | tf_op jit(solution)/shard_map/all_to_all | solution.py:244
  26.6 0.5 shard_map.102
  27.1 21.9 %all_to_all.20 = bf16[8,16,256]{2,1,0:T(8,128)(2,1)S(1)} all-to-all(bf16[8,16,256]{2,1,0:T(8,128)(2,1)S(1)} %broadcast_in_dim.16), channel_id=1, replica_groups=mesh['yh'=2,'core'=2,'y1'=2,'y0'=2,'zh'=8,'z0'=2,'x1'=2,'x0'=2] {'zh'}, dimensions={0} | all-to-all | bytes 131072 | tf_op jit(solution)/shard_map/all_to_all | solution.py:244
  49.0 12.3 %all_to_all.21 = bf16[4,8,16,256]{3,2,1,0:T(8,128)(2,1)S(1)} all-to-all(bf16[4,8,16,256]{3,2,1,0:T(8,128)(2,1)S(1)} %broadcast_in_dim.34), channel_id=1, replica_groups={{0,2,128,130},{1,3,129,131},{4,6,132,134},{5,7,133,135},{8,10,136,138},..., dimensions={0} | all-to-all | bytes 524288 | tf_op jit(solution)/shard_map/all_to_all | solution.py:244
  61.4 0.2 broadcast_in_dim.35
  61.6 0.0 copy-start
  61.6 0.0 copy-start.1
  61.6 0.0 copy-start.2
  61.6 21.9 %all_to_all.22 = bf16[8,4,8,16,256]{4,3,2,1,0:T(8,128)(2,1)S(1)} all-to-all(bf16[8,4,8,16,256]{4,3,2,1,0:T(8,128)(2,1)S(1)} %broadcast_in_dim.35), channel_id=1, replica_groups={{0,1,4,5,64,65,68,69},{2,3,6,7,66,67,70,71},{8,9,12,13,72,73,76,77},{10..., dimensions={0} | all-to-all | bytes 4194304 | tf_op jit(solution)/shard_map/all_to_all | solution.py:244
  83.5 3.5 %collective-permute-start = (bf16[2,2,2,2,2,8,16,256]{7,6,5,4,3,2,1,0:T(8,128)(2,1)S(1)}, bf16[2,2,2,2,2,8,16,256]{7,6,5,4,3,2,1,0:T(8,128)(2,1)S(1)}, u32[]{:S(2)}, u32[]{:S(2)}) collective-permute-start(bf16[2,2,2,2,2,8,16,256]{7,6,5,4,3,2,1,0:T(8,128)(2,1)S(1)} %bitcast.9), channel_id=1, source_target_pairs={{0,256},{256,0},{1,257},{257,1},{2,258},{258,2},{3,259},{259,3},{4... | collective-permute-start | bytes 6291464 | tf_op jit(solution)/shard_map/ppermute | solution.py:261
  87.0 0.0 copy-done
  87.0 0.0 copy-done.1
  87.0 0.0 copy-done.2
  87.0 2.1 %shard_map.103 = (f32[192,4096]{1,0:T(8,128)S(1)}, bf16[192,4096]{1,0:T(8,128)(2,1)S(1)}, f32[192,1]{1,0:T(8,128)S(1)}, bf16[192,256]{1,0:T(8,128)(2,1)S(1)}, f32[16,512]{1,0:T(8,128)}, /*index=5*/f32[16,512]{1,0:T(8,128)}) custom-call(s32[1]{0:T(128)} %bitcast.core_ref, bf16[2,2,2,2,2,8,16,256]{7,6,5,4,3,2,1,0:T(8,128)(2,1)S(1)} %bitcast.10, ...), custom_call_target="tpu_custom_call" | custom-call | flops 900000000 | bytes 12000000 | tf_op jit(solution)/shard_map/pallas_call | solution.py:137
  89.1 1.7 %collective-permute-done.weight_ref = bf16[2,2,2,2,2,8,16,256]{7,6,5,4,3,2,1,0:T(8,128)(2,1)S(1)} collective-permute-done((bf16[2,2,2,2,2,8,16,256]{7,6,5,4,3,2,1,0:T(8,128)(2,1)S(1)}, bf16[2,2,2,2,2,8,16,256]{7,6,5,4,3,2,1,0:T(8,128)(2,1)S(1)}, u32[]{:S(2)}, u32[]{:S(2)}) %collective-permute-start) | collective-permute-done | bytes 2097184 | tf_op jit(solution)/shard_map/ppermute | solution.py:261
  90.8 3.0 %shard_map.104 = (bf16[192,512]{1,0:T(8,128)(2,1)}, bf16[192,4096]{1,0:T(8,128)(2,1)}) custom-call(s32[1]{0:T(128)} %bitcast.core_ref, bf16[2,2,2,2,2,8,16,256]{7,6,5,4,3,2,1,0:T(8,128)(2,1)S(1)} %collective-permute-done.weight_ref, bf16[192,512]{1,0:T(8,128)(2,1)S(1)} %bitcast.14, f32[192,4096]{1,0:T(8,128)S(1)} %get-tuple-element.16.back_ref, ...), custom_call_target="tpu_custom_call" | custom-call | flops 900000000 | bytes 12000000 | tf_op jit(solution)/shard_map/pallas_call | solution.py:194
  (4 shorter events, 0.0 us)
Async XLA Ops:
  2.0 24.6 %all-to-all-start = ((bf16[4,16,512]{2,1,0:T(8,128)(2,1)}), bf16[4,16,512]{2,1,0:T(8,128)(2,1)S(1)}, u32[]{:S(2)}, u32[]{:S(2)}) async-start(bf16[4,16,512]{2,1,0:T(8,128)(2,1)} %broadcast_in_dim.15), calls=%async_computation | async-start | bytes 131072 | tf_op jit(solution)/shard_map/all_to_all | solution.py:244
  61.6 25.4 %copy-start = (bf16[1,192,4096]{2,1,0:T(8,128)(2,1)S(1)}, bf16[1,192,4096]{2,1,0:T(8,128)(2,1)}, u32[]{:S(2)}) copy-start(bf16[1,192,4096]{2,1,0:T(8,128)(2,1)} %param.7) | copy-start | bytes 4718596
  61.6 25.4 %copy-start.1 = (bf16[1,192,512]{2,1,0:T(8,128)(2,1)S(1)}, bf16[1,192,512]{2,1,0:T(8,128)(2,1)}, u32[]{:S(2)}) copy-start(bf16[1,192,512]{2,1,0:T(8,128)(2,1)} %param.9) | copy-start | bytes 589828
  61.6 25.4 %copy-start.2 = (f32[1,4096]{1,0:T(1,128)S(1)}, f32[1,4096]{1,0:T(1,128)}, u32[]{:S(2)}) copy-start(f32[1,4096]{1,0:T(1,128)} %gain_ref.3) | copy-start | bytes 49156
  83.5 7.3 %collective-permute-start = (bf16[2,2,2,2,2,8,16,256]{7,6,5,4,3,2,1,0:T(8,128)(2,1)S(1)}, bf16[2,2,2,2,2,8,16,256]{7,6,5,4,3,2,1,0:T(8,128)(2,1)S(1)}, u32[]{:S(2)}, u32[]{:S(2)}) collective-permute-start(bf16[2,2,2,2,2,8,16,256]{7,6,5,4,3,2,1,0:T(8,128)(2,1)S(1)} %bitcast.9), channel_id=1, source_target_pairs={{0,256},{256,0},{1,257},{257,1},{2,258},{258,2},{3,259},{259,3},{4... | collective-permute-start | bytes 6291464 | tf_op jit(solution)/shard_map/ppermute | solution.py:261

commit v8 on v7

--- a/solution.py
+++ b/solution.py
@@ -88,7 +88,7 @@
 
 
 CHUNK = 512
-PIECE_AXES = ("y0", "z0", "x0", "y1", "x1", "zh")
+PIECE_AXES = ("y0", "z0", "x0", "y1", "zh", "x1")
 
 
 def pieces_of(chunk, row_count):
@@ -214,14 +214,13 @@
     return (((y // 4 * 2 + core) * 4 + y % 4) * 16 + z) * 4 + x
 
 
-def squares():
+def pairs():
     groups = []
     for core in range(2):
         for y in (0, 1, 4, 5):
-            pair = (y, (y + 2 - 4 * core) % 8)
             for z in range(16):
-                for x in range(2):
-                    groups.append([place(core, y_at, z, x_at) for y_at in pair for x_at in (x, x + 2)])
+                for x in range(4):
+                    groups.append([place(core, y_at, z, x) for y_at in (y, (y + 2 - 4 * core) % 8)])
     return groups
 
 
@@ -254,8 +253,8 @@
     half = width // 2
     core = lax.axis_index("core")
     mine = jnp.where(core == 0, weight_part[:, :half], weight_part[:, half:])
-    got = gather(mine, ("zh",), 8)
-    got = gather(got, AXES, 4, squares())
+    got = gather(mine, ("zh", "x1"), 16)
+    got = gather(got, AXES, 2, pairs())
     got = gather(got, AXES, 8, cubes())
     got = got.reshape(tuple(SIZES[axis] for axis in PIECE_AXES) + (row_count, half))
     other = lax.ppermute(got, "core", [(0, 1), (1, 0)])

time: 94.3 us -> 97.2 us (1.031)
  blocking collectives: 56.1 us -> 60 us
    all_to_all x3, blocking collectives: 56.1 us -> 60 us  [gather(): lax.all_to_all(copies, axes, 0, 0, axis_index_groups=groups, tiled=True)]
where the time goes in v8:
time: 97.2 us; the launch traced here: 96.7 us
  blocking collectives  60 us (62%)
  starting transfers between devices  20 us (21%)
  waiting for transfers between devices  7.36 us (8%)
  Pallas kernels  5.58 us (6%)
  local copies, waits for them, and re-layouts  1.6 us (2%)
  other arithmetic  1.47 us (2%)
    all_to_all x3, blocking collectives, gather(): lax.all_to_all(copies, axes, 0, 0, axis_index_groups=groups, tiled=True)  60 us
    all_to_all x1, starting transfers between devices, gather(): lax.all_to_all(copies, axes, 0, 0, axis_index_groups=groups, tiled=True)  17.4 us
    all_to_all x1, waiting for transfers between devices, gather(): lax.all_to_all(copies, axes, 0, 0, axis_index_groups=groups, tiled=True)  5.69 us
    pallas_call x1, Pallas kernels, tail(): pl.pallas_call(tail_kernel, out_shape=(jax.ShapeDtypeStruct((count, 2 * h...  3.02 us
    ppermute x1, starting transfers between devices, body(): other = lax.ppermute(got, 'core', [(0, 1), (1, 0)])  2.61 us
    pallas_call x1, Pallas kernels, own_half(): pl.pallas_call(own_kernel, out_shape=(jax.ShapeDtypeStruct((count, width)...  2.07 us
  transfers between devices with their start and end apart: 2, of which 2 were waited for; matrix products, arithmetic and copies ran while one was open for 2% of the time, Pallas kernels for 2%

profile of v8, /device:TPU:1, one launch (start us, length us, event | category | flops | bytes accessed | tf_op | source)
XLA Modules:
  0.0 96.7 jit_solution(9335222629979030767)
XLA Ops:
  0.6 1.4 %broadcast_in_dim.15 = bf16[4,16,512]{2,1,0:T(8,128)(2,1)} broadcast(bf16[16,512]{1,0:T(8,128)(2,1)} %bitcast.17), dimensions={1,2} | broadcast | bytes 81920 | tf_op jit(solution)/shard_map/broadcast_in_dim | solution.py:242
  2.0 17.4 %all-to-all-start = ((bf16[4,16,512]{2,1,0:T(8,128)(2,1)}), bf16[4,16,512]{2,1,0:T(8,128)(2,1)S(1)}, u32[]{:S(2)}, u32[]{:S(2)}) async-start(bf16[4,16,512]{2,1,0:T(8,128)(2,1)} %broadcast_in_dim.15), calls=%async_computation | async-start | bytes 131072 | tf_op jit(solution)/shard_map/all_to_all | solution.py:243
  19.4 0.7 add_convert_fusion
  20.1 0.8 pad_maximum_fusion.held_ref
  20.9 5.7 %all-to-all-done.local_ref = bf16[4,16,512]{2,1,0:T(8,128)(2,1)S(1)} async-done(((bf16[4,16,512]{2,1,0:T(8,128)(2,1)}), bf16[4,16,512]{2,1,0:T(8,128)(2,1)S(1)}, u32[]{:S(2)}, u32[]{:S(2)}) %all-to-all-start) | async-done | bytes 65568 | tf_op jit(solution)/shard_map/all_to_all | solution.py:243
  26.6 0.5 shard_map.102
  27.1 27.5 %all_to_all.20 = bf16[16,16,256]{2,1,0:T(8,128)(2,1)S(1)} all-to-all(bf16[16,16,256]{2,1,0:T(8,128)(2,1)S(1)} %broadcast_in_dim.16), channel_id=1, replica_groups=mesh['yh'=2,'core'=2,'y1'=2,'y0'=2,'zh'=8,'z0'=2,'x1'=2,'x0'=2] {'zh','x1'}, dimensions={0} | all-to-all | bytes 262144 | tf_op jit(solution)/shard_map/all_to_all | solution.py:243
  54.6 8.6 %all_to_all.21 = bf16[2,16,16,256]{3,2,1,0:T(8,128)(2,1)S(1)} all-to-all(bf16[2,16,16,256]{3,2,1,0:T(8,128)(2,1)S(1)} %broadcast_in_dim.34), channel_id=1, replica_groups={{0,128},{1,129},{2,130},{3,131},{4,132},{5,133},{6,134},{7,135},{8,136}..., dimensions={0} | all-to-all | bytes 524288 | tf_op jit(solution)/shard_map/all_to_all | solution.py:243
  63.3 0.2 broadcast_in_dim.35
  63.5 0.0 copy-start
  63.5 0.0 copy-start.1
  63.5 0.0 copy-start.2
  63.5 23.8 %all_to_all.22 = bf16[8,2,16,16,256]{4,3,2,1,0:T(8,128)(2,1)S(1)} all-to-all(bf16[8,2,16,16,256]{4,3,2,1,0:T(8,128)(2,1)S(1)} %broadcast_in_dim.35), channel_id=1, replica_groups={{0,1,4,5,64,65,68,69},{2,3,6,7,66,67,70,71},{8,9,12,13,72,73,76,77},{10..., dimensions={0} | all-to-all | bytes 4194304 | tf_op jit(solution)/shard_map/all_to_all | solution.py:243
  87.3 2.6 %collective-permute-start = (bf16[2,2,2,2,8,2,16,256]{7,6,5,4,3,2,1,0:T(8,128)(2,1)S(1)}, bf16[2,2,2,2,8,2,16,256]{7,6,5,4,3,2,1,0:T(8,128)(2,1)S(1)}, u32[]{:S(2)}, u32[]{:S(2)}) collective-permute-start(bf16[2,2,2,2,8,2,16,256]{7,6,5,4,3,2,1,0:T(8,128)(2,1)S(1)} %bitcast.9), channel_id=1, source_target_pairs={{0,256},{256,0},{1,257},{257,1},{2,258},{258,2},{3,259},{259,3},{4... | collective-permute-start | bytes 6291464 | tf_op jit(solution)/shard_map/ppermute | solution.py:260
  89.9 0.0 copy-done
  89.9 0.0 copy-done.1
  90.0 0.0 copy-done.2
  90.0 2.1 %shard_map.103 = (f32[192,4096]{1,0:T(8,128)S(1)}, bf16[192,4096]{1,0:T(8,128)(2,1)S(1)}, f32[192,1]{1,0:T(8,128)S(1)}, bf16[192,256]{1,0:T(8,128)(2,1)S(1)}, f32[16,512]{1,0:T(8,128)}, /*index=5*/f32[16,512]{1,0:T(8,128)}) custom-call(s32[1]{0:T(128)} %bitcast.core_ref, bf16[2,2,2,2,8,2,16,256]{7,6,5,4,3,2,1,0:T(8,128)(2,1)S(1)} %bitcast.10, ...), custom_call_target="tpu_custom_call" | custom-call | flops 900000000 | bytes 12000000 | tf_op jit(solution)/shard_map/pallas_call | solution.py:137
  92.0 1.7 %collective-permute-done.weight_ref = bf16[2,2,2,2,8,2,16,256]{7,6,5,4,3,2,1,0:T(8,128)(2,1)S(1)} collective-permute-done((bf16[2,2,2,2,8,2,16,256]{7,6,5,4,3,2,1,0:T(8,128)(2,1)S(1)}, bf16[2,2,2,2,8,2,16,256]{7,6,5,4,3,2,1,0:T(8,128)(2,1)S(1)}, u32[]{:S(2)}, u32[]{:S(2)}) %collective-permute-start) | collective-permute-done | bytes 2097184 | tf_op jit(solution)/shard_map/ppermute | solution.py:260
  93.7 3.0 %shard_map.104 = (bf16[192,512]{1,0:T(8,128)(2,1)}, bf16[192,4096]{1,0:T(8,128)(2,1)}) custom-call(s32[1]{0:T(128)} %bitcast.core_ref, bf16[2,2,2,2,8,2,16,256]{7,6,5,4,3,2,1,0:T(8,128)(2,1)S(1)} %collective-permute-done.weight_ref, bf16[192,512]{1,0:T(8,128)(2,1)S(1)} %bitcast.14, f32[192,4096]{1,0:T(8,128)S(1)} %get-tuple-element.16.back_ref, ...), custom_call_target="tpu_custom_call" | custom-call | flops 900000000 | bytes 12000000 | tf_op jit(solution)/shard_map/pallas_call | solution.py:194
  (4 shorter events, 0.0 us)
Async XLA Ops:
  2.0 24.6 %all-to-all-start = ((bf16[4,16,512]{2,1,0:T(8,128)(2,1)}), bf16[4,16,512]{2,1,0:T(8,128)(2,1)S(1)}, u32[]{:S(2)}, u32[]{:S(2)}) async-start(bf16[4,16,512]{2,1,0:T(8,128)(2,1)} %broadcast_in_dim.15), calls=%async_computation | async-start | bytes 131072 | tf_op jit(solution)/shard_map/all_to_all | solution.py:243
  63.5 26.5 %copy-start = (bf16[1,192,4096]{2,1,0:T(8,128)(2,1)S(1)}, bf16[1,192,4096]{2,1,0:T(8,128)(2,1)}, u32[]{:S(2)}) copy-start(bf16[1,192,4096]{2,1,0:T(8,128)(2,1)} %param.7) | copy-start | bytes 4718596
  63.5 26.5 %copy-start.1 = (bf16[1,192,512]{2,1,0:T(8,128)(2,1)S(1)}, bf16[1,192,512]{2,1,0:T(8,128)(2,1)}, u32[]{:S(2)}) copy-start(bf16[1,192,512]{2,1,0:T(8,128)(2,1)} %param.9) | copy-start | bytes 589828
  63.5 26.5 %copy-start.2 = (f32[1,4096]{1,0:T(1,128)S(1)}, f32[1,4096]{1,0:T(1,128)}, u32[]{:S(2)}) copy-start(f32[1,4096]{1,0:T(1,128)} %gain_ref.3) | copy-start | bytes 49156
  87.3 6.4 %collective-permute-start = (bf16[2,2,2,2,8,2,16,256]{7,6,5,4,3,2,1,0:T(8,128)(2,1)S(1)}, bf16[2,2,2,2,8,2,16,256]{7,6,5,4,3,2,1,0:T(8,128)(2,1)S(1)}, u32[]{:S(2)}, u32[]{:S(2)}) collective-permute-start(bf16[2,2,2,2,8,2,16,256]{7,6,5,4,3,2,1,0:T(8,128)(2,1)S(1)} %bitcast.9), channel_id=1, source_target_pairs={{0,256},{256,0},{1,257},{257,1},{2,258},{258,2},{3,259},{259,3},{4... | collective-permute-start | bytes 6291464 | tf_op jit(solution)/shard_map/ppermute | solution.py:260

commit v9 on v7

--- a/solution.py
+++ b/solution.py
@@ -88,6 +88,7 @@
 
 
 CHUNK = 512
+ROWS = 48
 PIECE_AXES = ("y0", "z0", "x0", "y1", "x1", "zh")
 
 
@@ -172,15 +173,18 @@
             total = total + product[:, at : at + HB]
     keys_ref[:, columns_of(core, half)] = mine_ref[...]
     keys_ref[:, columns_of(1 - core, half)] = keys.astype(jnp.bfloat16)
-    copies = [pltpu.make_async_copy(keys_ref, keys_out, sems.at[len(parts)])]
+    copies = [pltpu.make_async_copy(keys_ref, keys_out, sems.at[tokens // ROWS])]
     copies[0].start()
     inverse = inverse_ref[...]
     centre = inverse * jnp.sum(total, axis=1, keepdims=True) / width
     factor = inverse * inverse * centre
-    for chunk, columns in enumerate(parts):
-        grads = inverse * scaled_ref[:, columns] - factor * tokens_ref[:, columns].astype(jnp.float32)
-        grads_ref[:, columns] = grads.astype(jnp.bfloat16)
-        copy = pltpu.make_async_copy(grads_ref.at[:, columns], grads_out.at[:, columns], sems.at[chunk])
+    for step_at, first in enumerate(range(0, tokens, ROWS)):
+        block = slice(first, first + ROWS)
+        for columns in parts:
+            values = tokens_ref[block, columns].astype(jnp.float32)
+            grads = inverse[block] * scaled_ref[block, columns] - factor[block] * values
+            grads_ref[block, columns] = grads.astype(jnp.bfloat16)
+        copy = pltpu.make_async_copy(grads_ref.at[block, :], grads_out.at[block, :], sems.at[step_at])
         copy.start()
         copies.append(copy)
     for copy in copies:
@@ -203,7 +207,7 @@
             pltpu.VMEM((count, width), jnp.float32),
             pltpu.VMEM((count, 2 * half), jnp.bfloat16),
             pltpu.VMEM((count, width), jnp.bfloat16),
-            pltpu.SemaphoreType.DMA((width // CHUNK + 1,)),
+            pltpu.SemaphoreType.DMA((count // ROWS + 1,)),
         ],
         compiler_params=pltpu.CompilerParams(vmem_limit_bytes=20 * 1024 * 1024),
         cost_estimate=pl.CostEstimate(flops=900_000_000, bytes_accessed=12_000_000, transcendentals=0),
@@ -212,17 +216,6 @@
 
 def place(core, y, z, x):
     return (((y // 4 * 2 + core) * 4 + y % 4) * 16 + z) * 4 + x
-
-
-def squares():
-    groups = []
-    for core in range(2):
-        for y in (0, 1, 4, 5):
-            pair = (y, (y + 2 - 4 * core) % 8)
-            for z in range(16):
-                for x in range(2):
-                    groups.append([place(core, y_at, z, x_at) for y_at in pair for x_at in (x, x + 2)])
-    return groups
 
 
 def cubes():
@@ -255,7 +248,7 @@
     core = lax.axis_index("core")
     mine = jnp.where(core == 0, weight_part[:, :half], weight_part[:, half:])
     got = gather(mine, ("zh",), 8)
-    got = gather(got, AXES, 4, squares())
+    got = gather(got, ("y1", "x1"), 4)
     got = gather(got, AXES, 8, cubes())
     got = got.reshape(tuple(SIZES[axis] for axis in PIECE_AXES) + (row_count, half))
     other = lax.ppermute(got, "core", [(0, 1), (1, 0)])

time: 94.3 us -> 94 us (level)
  no operation moved by 1% of the time
where the time goes in v9:
time: 94 us; the launch traced here: 93.5 us
  blocking collectives  56.3 us (60%)
  starting transfers between devices  20.7 us (22%)
  waiting for transfers between devices  7.36 us (8%)
  Pallas kernels  5.33 us (6%)
  local copies, waits for them, and re-layouts  1.63 us (2%)
  other arithmetic  1.47 us (2%)
    all_to_all x3, blocking collectives, gather(): lax.all_to_all(copies, axes, 0, 0, axis_index_groups=groups, tiled=True)  56.3 us
    all_to_all x1, starting transfers between devices, gather(): lax.all_to_all(copies, axes, 0, 0, axis_index_groups=groups, tiled=True)  17.4 us
    all_to_all x1, waiting for transfers between devices, gather(): lax.all_to_all(copies, axes, 0, 0, axis_index_groups=groups, tiled=True)  5.69 us
    ppermute x1, starting transfers between devices, body(): other = lax.ppermute(got, 'core', [(0, 1), (1, 0)])  3.31 us
    pallas_call x1, Pallas kernels, tail(): pl.pallas_call(tail_kernel, out_shape=(jax.ShapeDtypeStruct((count, 2 * h...  2.77 us
    pallas_call x1, Pallas kernels, own_half(): pl.pallas_call(own_kernel, out_shape=(jax.ShapeDtypeStruct((count, width)...  2.07 us
  transfers between devices with their start and end apart: 2, of which 2 were waited for; matrix products, arithmetic and copies ran while one was open for 2% of the time, Pallas kernels for 2%

profile of v9, /device:TPU:1, one launch (start us, length us, event | category | flops | bytes accessed | tf_op | source)
XLA Modules:
  0.0 93.5 jit_solution(12268134630678036488)
XLA Ops:
  0.6 1.4 %broadcast_in_dim.15 = bf16[4,16,512]{2,1,0:T(8,128)(2,1)} broadcast(bf16[16,512]{1,0:T(8,128)(2,1)} %bitcast.17), dimensions={1,2} | broadcast | bytes 81920 | tf_op jit(solution)/shard_map/broadcast_in_dim | solution.py:236
  2.0 17.4 %all-to-all-start = ((bf16[4,16,512]{2,1,0:T(8,128)(2,1)}), bf16[4,16,512]{2,1,0:T(8,128)(2,1)S(1)}, u32[]{:S(2)}, u32[]{:S(2)}) async-start(bf16[4,16,512]{2,1,0:T(8,128)(2,1)} %broadcast_in_dim.15), calls=%async_computation | async-start | bytes 131072 | tf_op jit(solution)/shard_map/all_to_all | solution.py:237
  19.4 0.7 add_convert_fusion
  20.1 0.8 pad_maximum_fusion.held_ref
  20.9 5.7 %all-to-all-done.local_ref = bf16[4,16,512]{2,1,0:T(8,128)(2,1)S(1)} async-done(((bf16[4,16,512]{2,1,0:T(8,128)(2,1)}), bf16[4,16,512]{2,1,0:T(8,128)(2,1)S(1)}, u32[]{:S(2)}, u32[]{:S(2)}) %all-to-all-start) | async-done | bytes 65568 | tf_op jit(solution)/shard_map/all_to_all | solution.py:237
  26.6 0.5 shard_map.102
  27.1 21.9 %all_to_all.20 = bf16[8,16,256]{2,1,0:T(8,128)(2,1)S(1)} all-to-all(bf16[8,16,256]{2,1,0:T(8,128)(2,1)S(1)} %broadcast_in_dim.16), channel_id=1, replica_groups=mesh['yh'=2,'core'=2,'y1'=2,'y0'=2,'zh'=8,'z0'=2,'x1'=2,'x0'=2] {'zh'}, dimensions={0} | all-to-all | bytes 131072 | tf_op jit(solution)/shard_map/all_to_all | solution.py:237
  49.0 12.5 %all_to_all.21 = bf16[4,8,16,256]{3,2,1,0:T(8,128)(2,1)S(1)} all-to-all(bf16[4,8,16,256]{3,2,1,0:T(8,128)(2,1)S(1)} %broadcast_in_dim.34), channel_id=1, replica_groups=mesh['yh'=2,'core'=2,'y1'=2,'y0'=2,'zh'=8,'z0'=2,'x1'=2,'x0'=2] {'y1','x1'}, dimensions={0} | all-to-all | bytes 524288 | tf_op jit(solution)/shard_map/all_to_all | solution.py:237
  61.6 0.2 broadcast_in_dim.35
  61.8 0.0 copy-start
  61.8 0.0 copy-start.1
  61.8 0.0 copy-start.2
  61.8 21.9 %all_to_all.22 = bf16[8,4,8,16,256]{4,3,2,1,0:T(8,128)(2,1)S(1)} all-to-all(bf16[8,4,8,16,256]{4,3,2,1,0:T(8,128)(2,1)S(1)} %broadcast_in_dim.35), channel_id=1, replica_groups={{0,1,4,5,64,65,68,69},{2,3,6,7,66,67,70,71},{8,9,12,13,72,73,76,77},{10..., dimensions={0} | all-to-all | bytes 4194304 | tf_op jit(solution)/shard_map/all_to_all | solution.py:237
  83.7 3.3 %collective-permute-start = (bf16[2,2,2,2,2,8,16,256]{7,6,5,4,3,2,1,0:T(8,128)(2,1)S(1)}, bf16[2,2,2,2,2,8,16,256]{7,6,5,4,3,2,1,0:T(8,128)(2,1)S(1)}, u32[]{:S(2)}, u32[]{:S(2)}) collective-permute-start(bf16[2,2,2,2,2,8,16,256]{7,6,5,4,3,2,1,0:T(8,128)(2,1)S(1)} %bitcast.9), channel_id=1, source_target_pairs={{0,256},{256,0},{1,257},{257,1},{2,258},{258,2},{3,259},{259,3},{4... | collective-permute-start | bytes 6291464 | tf_op jit(solution)/shard_map/ppermute | solution.py:254
  87.0 0.0 copy-done
  87.0 0.0 copy-done.1
  87.0 0.0 copy-done.2
  87.0 2.1 %shard_map.103 = (f32[192,4096]{1,0:T(8,128)S(1)}, bf16[192,4096]{1,0:T(8,128)(2,1)S(1)}, f32[192,1]{1,0:T(8,128)S(1)}, bf16[192,256]{1,0:T(8,128)(2,1)S(1)}, f32[16,512]{1,0:T(8,128)}, /*index=5*/f32[16,512]{1,0:T(8,128)}) custom-call(s32[1]{0:T(128)} %bitcast.core_ref, bf16[2,2,2,2,2,8,16,256]{7,6,5,4,3,2,1,0:T(8,128)(2,1)S(1)} %bitcast.10, ...), custom_call_target="tpu_custom_call" | custom-call | flops 900000000 | bytes 12000000 | tf_op jit(solution)/shard_map/pallas_call | solution.py:138
  89.1 1.7 %collective-permute-done.weight_ref = bf16[2,2,2,2,2,8,16,256]{7,6,5,4,3,2,1,0:T(8,128)(2,1)S(1)} collective-permute-done((bf16[2,2,2,2,2,8,16,256]{7,6,5,4,3,2,1,0:T(8,128)(2,1)S(1)}, bf16[2,2,2,2,2,8,16,256]{7,6,5,4,3,2,1,0:T(8,128)(2,1)S(1)}, u32[]{:S(2)}, u32[]{:S(2)}) %collective-permute-start) | collective-permute-done | bytes 2097184 | tf_op jit(solution)/shard_map/ppermute | solution.py:254
  90.8 2.8 %shard_map.104 = (bf16[192,512]{1,0:T(8,128)(2,1)}, bf16[192,4096]{1,0:T(8,128)(2,1)}) custom-call(s32[1]{0:T(128)} %bitcast.core_ref, bf16[2,2,2,2,2,8,16,256]{7,6,5,4,3,2,1,0:T(8,128)(2,1)S(1)} %collective-permute-done.weight_ref, bf16[192,512]{1,0:T(8,128)(2,1)S(1)} %bitcast.14, f32[192,4096]{1,0:T(8,128)S(1)} %get-tuple-element.16.back_ref, ...), custom_call_target="tpu_custom_call" | custom-call | flops 900000000 | bytes 12000000 | tf_op jit(solution)/shard_map/pallas_call | solution.py:198
  (4 shorter events, 0.0 us)
Async XLA Ops:
  2.0 24.6 %all-to-all-start = ((bf16[4,16,512]{2,1,0:T(8,128)(2,1)}), bf16[4,16,512]{2,1,0:T(8,128)(2,1)S(1)}, u32[]{:S(2)}, u32[]{:S(2)}) async-start(bf16[4,16,512]{2,1,0:T(8,128)(2,1)} %broadcast_in_dim.15), calls=%async_computation | async-start | bytes 131072 | tf_op jit(solution)/shard_map/all_to_all | solution.py:237
  61.8 25.2 %copy-start = (bf16[1,192,4096]{2,1,0:T(8,128)(2,1)S(1)}, bf16[1,192,4096]{2,1,0:T(8,128)(2,1)}, u32[]{:S(2)}) copy-start(bf16[1,192,4096]{2,1,0:T(8,128)(2,1)} %param.7) | copy-start | bytes 4718596
  61.8 25.2 %copy-start.1 = (bf16[1,192,512]{2,1,0:T(8,128)(2,1)S(1)}, bf16[1,192,512]{2,1,0:T(8,128)(2,1)}, u32[]{:S(2)}) copy-start(bf16[1,192,512]{2,1,0:T(8,128)(2,1)} %param.9) | copy-start | bytes 589828
  61.8 25.2 %copy-start.2 = (f32[1,4096]{1,0:T(1,128)S(1)}, f32[1,4096]{1,0:T(1,128)}, u32[]{:S(2)}) copy-start(f32[1,4096]{1,0:T(1,128)} %gain_ref.3) | copy-start | bytes 49156
  83.7 7.1 %collective-permute-start = (bf16[2,2,2,2,2,8,16,256]{7,6,5,4,3,2,1,0:T(8,128)(2,1)S(1)}, bf16[2,2,2,2,2,8,16,256]{7,6,5,4,3,2,1,0:T(8,128)(2,1)S(1)}, u32[]{:S(2)}, u32[]{:S(2)}) collective-permute-start(bf16[2,2,2,2,2,8,16,256]{7,6,5,4,3,2,1,0:T(8,128)(2,1)S(1)} %bitcast.9), channel_id=1, source_target_pairs={{0,256},{256,0},{1,257},{257,1},{2,258},{258,2},{3,259},{259,3},{4... | collective-permute-start | bytes 6291464 | tf_op jit(solution)/shard_map/ppermute | solution.py:254
